TPU v7x, 32 devices: a whole 2x2x4 slice. The times are simulated.
32 devices in a mesh: grp: 2 (over y), gx: 16 (over z, x, core).
Axes of the slice: x: 2, y: 2, z: 4, core: 2. Of those that a mesh axis runs over, the one named last changes fastest.
Arguments:
- mesh_feature_array: bfloat16 [128, 32, 32, 512], P(('grp', 'gx')), parts along dimension 0, may hold values from -6 to 6
- stencil_coefficients: float32 [27, 512], replicated, may hold values from -1.25 to 1.25
- partition_affinity_matrix: bfloat16 [512, 512], replicated, may hold values from -16 to 16
- softness_mapping_matrix: float32 [512], replicated, may hold values from -0.25 to 0.25
- content_mapping_matrix: bfloat16 [512, 512], replicated, may hold values from -0.25 to 0.25
- layernorm_multiplier: float32 [512], replicated, may hold values from 0.1 to 1.9
- widening_matrix: bfloat16 [512, 1024], replicated, may hold values from -0.25 to 0.25
- narrowing_matrix: bfloat16 [1024, 512], replicated, may hold values from -0.1875 to 0.1875
- final_mapping_matrix: bfloat16 [512, 512], replicated, may hold values from -0.25 to 0.25
Outputs:
- updated: bfloat16 [128, 32, 32, 512], P(('grp', 'gx')), parts along dimension 0
- slice_out: bfloat16 [1024, 512], P(('grp', 'gx')), parts along dimension 0
There are 2 independent parts, one for each index of `grp`. A program takes and returns all parts, laid end to end along the dimension named above; an argument that names none is the same for every part. Nothing has to cross between parts.
All inputs are finite; a program needn't handle non-finite values.
Results may differ from a plain program's by a relative error of at most 0.0056.
Values may be sent and summed in bfloat16 or wider, within the bound.
No kernel may reach another device: no remote copies, remote signals or barrier semaphores. Data moves between devices by JAX's collectives and lax.ppermute only.
A program may use at most 128 MiB of HBM per device.

v0:
```python
import functools
import math

import jax
import jax.numpy as jnp
from jax import lax
from jax.experimental import pallas as pl
from jax.experimental.pallas import tpu as pltpu
from jax.sharding import PartitionSpec as P

epsilon = 1e-05
LANES = 128
BLOCK = 256
GROUP = 8
TILE = 16
REPEAT = 8
MIB = 2**20
LIMIT = 32 * MIB
F32, BF16 = jnp.float32, jnp.bfloat16
CONV = BF16
VMEM = pl.BlockSpec(memory_space=pltpu.VMEM)
SMEM = pl.BlockSpec(memory_space=pltpu.SMEM)
HBM = pl.BlockSpec(memory_space=pltpu.HBM)


def dot(a, b):
    return jnp.dot(a, b, preferred_element_type=F32)


def gelu(x):
    inner = x * (x * x * (0.044715 * math.sqrt(2 / math.pi)) + math.sqrt(2 / math.pi))
    return x + x * jnp.tanh(inner)


def spread_taps(k_ref, planes, taps_ref):
    for role, plane in enumerate(planes):
        for tap in range(9):
            row = k_ref[pl.ds(9 * plane + tap, 1), :]
            taps_ref[9 * role + tap] = jnp.broadcast_to(row, taps_ref.shape[1:]).astype(CONV)


def conv_rows(sources, taps_ref, lanes, count, known=()):
    sums = [[None] * 3 for _ in range(count)]
    for role, rows in sources:
        taps = [taps_ref[9 * role + i, :, lanes] for i in range(9)]
        for j, row in enumerate(rows):
            if row is None:
                continue
            depth, width = row.shape
            row = row.astype(CONV).reshape(depth // REPEAT, REPEAT, width)
            for out in range(max(0, j - 2), min(count, j + 1)):
                for c in range(3):
                    term = row * taps[3 * (j - out) + c]
                    sums[out][c] = term if sums[out][c] is None else sums[out][c] + term
    for out, row in enumerate(known):
        sums[out][1] = sums[out][1] + row.astype(CONV).reshape(sums[out][1].shape)
    position = lax.broadcasted_iota(jnp.int32, (8, width), 0)
    results = []
    for out in range(count):
        before, here, after = (s.astype(F32).reshape(depth, width) for s in sums[out])
        before, after = pltpu.roll(before, 1, 0), pltpu.roll(after, depth - 1, 0)
        low = jnp.where(position == 0, 0.0, before[:8])
        high = jnp.where(position == 7, 0.0, after[depth - 8 :])
        before = jnp.concatenate([low, before[8:]], axis=0)
        after = jnp.concatenate([after[: depth - 8], high], axis=0)
        results.append(here + before + after)
    return results


def channel_blocks(channels):
    return [slice(i, i + BLOCK) for i in range(0, channels, BLOCK)]


def inner_row(ref, plane, y, lanes, inside=None):
    if inside is None:
        return ref[plane, y, :, lanes]
    row = ref[plane, jnp.clip(y, 0, ref.shape[1] - 1), :, lanes].astype(F32)
    return (row * jnp.where(inside, 1.0, 0.0)).astype(BF16)


def nt_dot(a, b):
    return lax.dot_general(a, b, (((1,), (1,)), ((), ())), preferred_element_type=F32)


def assign(hid, map_ref, mass_ref):
    cells = hid.shape[0]
    slices = map_ref.shape[0] - TILE
    raw = nt_dot(map_ref[...], hid)
    soft = raw[slices : slices + 8]
    temperature = 0.25 + jnp.maximum(soft, 0.0) + jnp.log(1.0 + jnp.exp(-jnp.abs(soft)))
    scale = (1.0 / math.log(2.0)) / temperature
    raw = raw[:slices].reshape(slices // 8, 8, cells)
    top = jnp.max(jnp.max(raw, axis=0), axis=0, keepdims=True)
    powers = jnp.exp2((raw - top[None]) * scale[None])
    total = jnp.sum(jnp.sum(powers, axis=0), axis=0, keepdims=True)
    probs = (powers * (1.0 / total)[None]).reshape(slices, cells)
    mass = probs[:, :LANES]
    for start in range(LANES, cells, LANES):
        mass = mass + probs[:, start : start + LANES]
    mass_ref[...] += mass
    return probs.astype(BF16)


def ends_kernel(me_ref, _, x_ref, k_ref, near_ref, partial_ref, taps_ref):
    planes, height, depth, channels = x_ref.shape
    odd = me_ref[0] & 1

    def row(y, carry):
        near_ref[0, y] = x_ref[(planes - 1) * (1 - odd), y]
        return carry

    lax.fori_loop(0, height, row, 0)
    spread_taps(k_ref, range(3), taps_ref)
    for which, known in enumerate((((1, 0), (2, 1)), ((0, planes - 2), (1, planes - 1)))):
        def put(y, lanes, rows, known=known, which=which):
            sources = [(role, [None if b is None else x_ref[p, y + b, :, lanes] for b in rows])
                       for role, p in known]
            totals = conv_rows(sources, taps_ref, lanes, len(rows) - 2)
            for i, total in enumerate(totals):
                start = (y + i) * depth
                start = start if isinstance(y, int) else pl.multiple_of(start, depth)
                partial_ref[which, pl.ds(start, depth), lanes] = total.astype(BF16)

        for lanes in channel_blocks(channels):
            put(0, lanes, (None, 0, 1))
            put(height - 1, lanes, (-1, 0, None))

        def pair(i, carry, put=put):
            for lanes in channel_blocks(channels):
                put(2 * i + 1, lanes, (-1, 0, 1, 2))
            return carry

        lax.fori_loop(0, (height - 2) // 2, pair, 0)


def ends_call(me, after, x, taps):
    planes, height, depth, channels = x.shape
    cells = height * depth
    return pl.pallas_call(
        ends_kernel,
        in_specs=[SMEM, pl.BlockSpec(memory_space=pl.ANY)] + [VMEM] * 2,
        out_specs=[VMEM] * 2,
        out_shape=[
            jax.ShapeDtypeStruct((1, height, depth, channels), BF16),
            jax.ShapeDtypeStruct((2, cells, channels), BF16),
        ],
        scratch_shapes=[pltpu.VMEM((27, REPEAT, channels), CONV)],
        cost_estimate=pl.CostEstimate(
            flops=cells * channels * 12000, bytes_accessed=8 * cells * channels, transcendentals=0
        ),
        compiler_params=pltpu.CompilerParams(vmem_limit_bytes=LIMIT),
        name="ends",
    )(me, after, x, taps)


def reverse_lowest(value, bits):
    return ((value & ((1 << (bits - 1)) - 1)) << 1) | (value >> (bits - 1))


def inside_kernel(bits, x_ref, k_ref, affinity_ref, softness_ref, probs_ref, sums_ref, mass_ref, map_ref,
                  taps_ref, even_ref, odd_ref, hid_ref, by_slice_ref):
    planes, height, depth, channels = x_ref.shape
    slices = affinity_ref.shape[1]
    spread_taps(k_ref, range(3), taps_ref)
    run = slices >> bits
    new = lax.broadcasted_iota(jnp.int32, (slices, 1), 0)
    old = lax.broadcasted_iota(jnp.int32, (slices, slices), 1)
    place = new & (run - 1)
    owner = reverse_lowest(new >> (run.bit_length() - 1), bits)
    order = (old == owner * run + place).astype(BF16)
    map_ref[:slices] = (0.5 * nt_dot(order, affinity_ref[...])).astype(BF16)
    softness = softness_ref[...].astype(BF16).astype(F32)
    map_ref[slices:] = jnp.broadcast_to(0.5 * softness, (TILE, channels)).astype(BF16)

    sums_ref[...] = jnp.zeros(sums_ref.shape, F32)
    mass_ref[...] = jnp.zeros(mass_ref.shape, F32)
    groups = height // GROUP
    cells = GROUP * depth

    def conv(t, hid_ref):
        plane, first = t // groups, lax.rem(t, groups) * GROUP
        for lanes in channel_blocks(channels):
            for j in range(0, GROUP, 2):
                sources = []
                for role in range(3):
                    rows = []
                    for b in (-1, 0, 1, 2):
                        y, ok = first + j + b, None
                        if j + b < 0:
                            ok = first > 0
                        elif j + b >= GROUP:
                            ok = first + GROUP < height
                        rows.append(inner_row(x_ref, plane + role, y, lanes, ok))
                    sources.append((role, rows))
                for i, total in enumerate(conv_rows(sources, taps_ref, lanes, 2)):
                    hid_ref[(j + i) * depth : (j + i + 1) * depth, lanes] = gelu(total.astype(BF16))

    def share(t, source_ref, at):
        hid = source_ref[...]
        by_slice = assign(hid, map_ref, mass_ref)
        start = pl.multiple_of(lax.rem(t, groups) * cells, cells)
        probs_ref[t // groups, pl.ds(start, cells), :] = by_slice.T
        hid_ref[at, :] = hid
        by_slice_ref[:, at] = by_slice

    count = (planes - 2) * groups
    conv(jnp.int32(0), even_ref)

    def two(s, carry):
        t = 2 * s
        share(t, even_ref, slice(0, cells))
        conv(t + 1, odd_ref)
        share(t + 1, odd_ref, slice(cells, 2 * cells))
        sums_ref[...] += dot(by_slice_ref[...], hid_ref[...])
        conv(jnp.minimum(t + 2, count - 1), even_ref)
        return carry

    lax.fori_loop(0, count // 2, two, 0)


def inside_call(x, taps, affinity, softness, bits):
    planes, height, depth, channels = x.shape
    slices = affinity.shape[1]
    cells = height * depth
    work = planes * cells * channels
    return pl.pallas_call(
        functools.partial(inside_kernel, bits),
        in_specs=[VMEM] * 4,
        out_specs=[VMEM] * 4,
        out_shape=[
            jax.ShapeDtypeStruct((planes - 2, cells, slices), BF16),
            jax.ShapeDtypeStruct((slices, channels), F32),
            jax.ShapeDtypeStruct((slices, LANES), F32),
            jax.ShapeDtypeStruct((slices + TILE, channels), BF16),
        ],
        scratch_shapes=[
            pltpu.VMEM((27, REPEAT, channels), CONV),
            pltpu.VMEM((GROUP * depth, channels), BF16),
            pltpu.VMEM((GROUP * depth, channels), BF16),
            pltpu.VMEM((2 * GROUP * depth, channels), BF16),
            pltpu.VMEM((slices, 2 * GROUP * depth), BF16),
        ],
        cost_estimate=pl.CostEstimate(
            flops=work * 7000, bytes_accessed=2 * work, transcendentals=2 * work
        ),
        compiler_params=pltpu.CompilerParams(vmem_limit_bytes=LIMIT),
        name="inside",
    )(x, taps, affinity, softness)


def edge_kernel(is_far, me_ref, halo_ref, partial_ref, k_ref, map_ref, sums_in_ref, mass_in_ref, *rest):
    if is_far:
        by_slice_ref, send_ref, sums_ref, mass_ref, hid_ref, taps_ref = rest
    else:
        probs_ref, sums_ref, mass_ref, taps_ref, hid_ref, by_slice_ref = rest
    _, height, depth, channels = halo_ref.shape
    slices = sums_in_ref.shape[0]
    odd = me_ref[0] & 1
    side = odd if is_far else 1 - odd
    spread_taps(k_ref, [2 * side], taps_ref)
    mass_ref[...] = mass_in_ref[...]
    cells = GROUP * depth
    most = height * depth - cells

    def conv(first):
        for lanes in channel_blocks(channels):
            for y in range(first, first + GROUP, 2):
                rows = [halo_ref[0, y + b, :, lanes] if 0 <= y + b < height else None
                        for b in (-1, 0, 1, 2)]
                ats = [slice((y + i) * depth, (y + i + 1) * depth) for i in range(2)]
                known = [partial_ref[side, at, lanes] for at in ats]
                for at, total in zip(ats, conv_rows([(0, rows)], taps_ref, lanes, 2, known)):
                    hid_ref[at, lanes] = gelu(total.astype(BF16))

    conv(0)
    for first in range(0, height, GROUP):
        if first + GROUP < height:
            conv(first + GROUP)
        group = slice(first * depth, first * depth + cells)
        by_slice = assign(hid_ref[group], map_ref, mass_ref)
        if not is_far:
            probs_ref[0, group] = by_slice.T
        by_slice_ref[:, group] = by_slice
        if group.stop == most:
            sums_ref[...] = sums_in_ref[...] + dot(by_slice_ref[:, :most], hid_ref[:most])
    if not is_far:
        sums_ref[...] += dot(by_slice_ref[:, most:], hid_ref[most:])
        return
    write_share(1 - odd, cells, by_slice_ref, hid_ref, sums_ref, mass_ref, send_ref)


def write_share(side, left, by_slice_ref, hid_ref, sums_ref, mass_ref, share_ref):
    slices, channels = sums_ref.shape
    most = hid_ref.shape[0] - left
    owners, rows, _ = share_ref.shape
    held = channels // LANES
    rows = (rows - 8) // held
    start = pl.multiple_of(side * (slices // 2), slices // 2)
    mine = pl.ds(start, slices // 2)
    total = sums_ref[mine, :] + dot(by_slice_ref[mine, most:], hid_ref[most:])
    for i in range(held):
        part = total[:, i * LANES : (i + 1) * LANES].astype(share_ref.dtype)
        share_ref[:, i * rows : (i + 1) * rows, :] = part.reshape(owners, rows, LANES)
    tiles = rows // 8
    lane = lax.broadcasted_iota(jnp.int32, (8, LANES), 1)
    mass = mass_ref[mine, :]
    for owner in range(owners):
        tail = None
        for g in range(tiles):
            tile = mass[owner * rows + 8 * g : owner * rows + 8 * (g + 1)]
            width = LANES
            while width > LANES // tiles:
                width //= 2
                tile = tile + pltpu.roll(tile, width, 1)
            tail = tile if tail is None else jnp.where(lane >= g * width, tile, tail)
        share_ref[owner, held * rows :, :] = tail.astype(share_ref.dtype)


def keep_kernel(left, me_ref, by_slice_ref, hid_ref, sums_ref, mass_ref, keep_ref, probs_ref):
    write_share(me_ref[0] & 1, left, by_slice_ref, hid_ref, sums_ref, mass_ref, keep_ref)
    probs_ref[0] = by_slice_ref[...].T


def keep_call(me, by_slice, hid, sums, mass, shape, left):
    slices, cells = by_slice.shape
    return pl.pallas_call(
        functools.partial(keep_kernel, left),
        in_specs=[SMEM] + [VMEM] * 4,
        out_specs=[VMEM, VMEM],
        out_shape=[jax.ShapeDtypeStruct(shape, F32), jax.ShapeDtypeStruct((1, cells, slices), BF16)],
        cost_estimate=pl.CostEstimate(flops=2**28, bytes_accessed=2**21, transcendentals=0),
        compiler_params=pltpu.CompilerParams(vmem_limit_bytes=LIMIT),
        name="keep",
    )(me, by_slice, hid, sums, mass)


def edge_call(is_far, me, halo, taps, maps, partial, sums, mass, owners):
    _, height, depth, channels = halo.shape
    slices = sums.shape[0]
    cells = height * depth
    hidden, by_slice = ((cells, channels), BF16), ((slices, cells), BF16)
    carry = [(s.shape, F32) for s in (sums, mass)]
    scratch = [((9, REPEAT, channels), CONV)]
    if is_far:
        rows = channels // LANES * (slices // owners) + 8
        outs = [by_slice, ((owners // 2, rows, LANES), BF16)] + carry + [hidden]
    else:
        outs = [((1, cells, slices), BF16)] + carry
        scratch += [hidden, by_slice]
    return pl.pallas_call(
        functools.partial(edge_kernel, is_far),
        in_specs=[SMEM] + [VMEM] * 6,
        out_specs=[VMEM] * len(outs),
        out_shape=[jax.ShapeDtypeStruct(*o) for o in outs],
        scratch_shapes=[pltpu.VMEM(*o) for o in scratch],
        cost_estimate=pl.CostEstimate(
            flops=cells * channels * 16000, bytes_accessed=4 * cells * channels,
            transcendentals=2 * cells * channels,
        ),
        compiler_params=pltpu.CompilerParams(vmem_limit_bytes=LIMIT),
        name="far" if is_far else "near",
    )(me, halo, partial, taps, maps, sums, mass)


def merge_kernel(keep_ref, other_ref, out_ref):
    out_ref[...] = (keep_ref[...] + other_ref[...].astype(F32)).astype(BF16)


def merge_call(keep, other):
    return pl.pallas_call(
        merge_kernel,
        in_specs=[VMEM, VMEM],
        out_specs=VMEM,
        out_shape=jax.ShapeDtypeStruct(keep.shape, BF16),
        compiler_params=pltpu.CompilerParams(vmem_limit_bytes=LIMIT),
        name="merge",
    )(keep, other)


def owner_kernel(parts_ref, gain_ref, content_ref, widening_ref,
                 narrowing_ref, final_ref, out_ref, mapped_ref):
    channels = content_ref.shape[0]
    held = channels // LANES
    rows = out_ref.shape[0]
    total = jnp.sum(parts_ref[...].astype(F32), axis=0)
    pooled = jnp.concatenate([total[i * rows : (i + 1) * rows] for i in range(held)], axis=1)
    tail = total[held * rows :]
    lane = lax.broadcasted_iota(jnp.int32, (8, LANES), 1)
    width = LANES // (rows // 8)
    mass = jnp.concatenate([
        jnp.sum(jnp.where((lane >= g) & (lane < g + width), tail, 0.0), axis=1, keepdims=True)
        for g in range(0, LANES, width)
    ], axis=0)
    pooled = 0.5 * pooled / (mass + epsilon)
    high = pooled.astype(BF16)
    low = (pooled - high.astype(F32)).astype(BF16)
    tokens = dot(jnp.concatenate([high, low], axis=0), content_ref[...])
    tokens = tokens[:rows] + tokens[rows:]
    center = jnp.mean(tokens, axis=-1, keepdims=True)
    spread = jnp.mean((tokens - center) ** 2, axis=-1, keepdims=True)
    normed = ((tokens - center) * (1.0 / jnp.sqrt(spread + epsilon)) * gain_ref[...]).astype(BF16)
    inner = (0.5 * gelu(dot(normed, widening_ref[...]))).astype(BF16)
    out = (tokens + dot(inner, narrowing_ref[...])).astype(BF16)
    out_ref[...] = out
    mapped = dot(out, final_ref[...]).astype(BF16)
    mapped_ref[...] = jnp.broadcast_to(mapped[None], mapped_ref.shape)


def owner_call(parts, gain, *weights):
    channels = weights[0].shape[0]
    owners = parts.shape[0]
    rows = (parts.shape[1] - 8) // (channels // LANES)
    return pl.pallas_call(
        owner_kernel,
        in_specs=[VMEM] * 6,
        out_specs=[VMEM, VMEM],
        out_shape=[
            jax.ShapeDtypeStruct((rows, channels), BF16),
            jax.ShapeDtypeStruct((owners, rows, channels), BF16),
        ],
        compiler_params=pltpu.CompilerParams(vmem_limit_bytes=LIMIT),
        name="owner",
    )(parts, gain, *weights)


def ahead_kernel(me_ref, x_ref, inside_ref, near_ref, own_ref, out_ref):
    planes = x_ref.shape[0]
    half = own_ref.shape[0]
    odd = me_ref[0] & 1
    columns = pl.ds(pl.multiple_of(odd * half, half), half)

    def step(i, carry):
        change = dot(inside_ref[i, :, columns], own_ref[...])
        out_ref[i] = x_ref[i + 1].astype(F32) + change
        return carry

    lax.fori_loop(0, planes - 2, step, 0)
    change = dot(near_ref[0, :, columns], own_ref[...])
    out_ref[planes - 2] = x_ref[(planes - 1) * (1 - odd)].astype(F32) + change


def ahead_call(me, x, inside, near, own):
    planes, cells, channels = x.shape
    return pl.pallas_call(
        ahead_kernel,
        in_specs=[SMEM] + [VMEM] * 4,
        out_specs=VMEM,
        out_shape=jax.ShapeDtypeStruct((planes - 1, cells, channels), F32),
        cost_estimate=pl.CostEstimate(flops=2**30, bytes_accessed=2**23, transcendentals=0),
        compiler_params=pltpu.CompilerParams(vmem_limit_bytes=LIMIT),
        name="ahead",
    )(me, x, inside, near, own)


def update_kernel(me_ref, x_ref, ahead_ref, inside_ref, near_ref, far_ref, own_ref, other_ref, out_ref,
                  done_ref, mapped_ref, sem):
    planes, cells, channels = x_ref.shape
    half = own_ref.shape[0]
    odd = me_ref[0] & 1
    mine = pl.ds(pl.multiple_of(odd * half, half), half)
    others = pl.ds(pl.multiple_of((1 - odd) * half, half), half)
    mapped_ref[mine] = own_ref[...]
    mapped_ref[others] = other_ref[...]

    pieces = 2
    rows = cells // pieces
    near, far = (planes - 1) * (1 - odd), (planes - 1) * odd

    def store(plane, piece):
        at = pl.ds(pl.multiple_of(piece * rows, rows), rows)
        return pltpu.make_async_copy(
            done_ref.at[plane, at], out_ref.at[plane, at], sem.at[plane * pieces + piece]
        )

    def step(i, carry):
        part, piece = i // pieces, lax.rem(i, pieces)
        at = pl.ds(pl.multiple_of(piece * rows, rows), rows)
        total = ahead_ref[part, at, :] + dot(inside_ref[part, at, others], other_ref[...])
        done_ref[part + 1, at, :] = total.astype(BF16)
        store(part + 1, piece).start()
        return carry

    lax.fori_loop(0, (planes - 2) * pieces, step, 0)
    for piece in range(pieces):
        at = pl.ds(piece * rows, rows)
        total = ahead_ref[planes - 2, at, :] + dot(near_ref[0, at, others], other_ref[...])
        done_ref[near, at, :] = total.astype(BF16)
        store(near, piece).start()
    for piece in range(pieces):
        at = pl.ds(piece * rows, rows)
        change = dot(far_ref[0, at], mapped_ref[...])
        done_ref[far, at, :] = (x_ref[far, at, :].astype(F32) + change).astype(BF16)
        store(far, piece).start()

    def finish(i, carry):
        store(i // pieces, lax.rem(i, pieces)).wait()
        return carry

    lax.fori_loop(0, planes * pieces, finish, 0)


def update_call(me, x, ahead, inside, near, far, own, other):
    planes, cells, channels = x.shape
    return pl.pallas_call(
        update_kernel,
        in_specs=[SMEM] + [VMEM] * 7,
        out_specs=HBM,
        out_shape=jax.ShapeDtypeStruct(x.shape, BF16),
        scratch_shapes=[
            pltpu.VMEM(x.shape, BF16),
            pltpu.VMEM((2 * own.shape[0], channels), BF16),
            pltpu.SemaphoreType.DMA((2 * planes,)),
        ],
        compiler_params=pltpu.CompilerParams(vmem_limit_bytes=LIMIT),
        name="update",
    )(me, x, ahead, inside, near, far, own, other)


def per_device(
    mesh_feature_array,
    stencil_coefficients,
    partition_affinity_matrix,
    softness_mapping_matrix,
    content_mapping_matrix,
    layernorm_multiplier,
    widening_matrix,
    narrowing_matrix,
    final_mapping_matrix,
):
    x = mesh_feature_array
    planes, height, depth, channels = x.shape
    slices = partition_affinity_matrix.shape[1]
    n = lax.axis_size("gx")
    me = lax.axis_index("gx").astype(jnp.int32)[None]
    far_pairs = [p for i in range(1, n - 1, 2) for p in ((i, i + 1), (i + 1, i))]
    near_pairs = [p for i in range(0, n, 2) for p in ((i, i + 1), (i + 1, i))]
    far_plane = lax.dynamic_slice_in_dim(x, (planes - 1) * (me[0] & 1), 1)
    far_halo = lax.ppermute(far_plane, "gx", far_pairs)

    owners = min(n // 2, slices // 2 // TILE)
    share = n // 2 // owners
    groups = [[2 * (share * j + s) + h for j in range(owners)] for h in range(2) for s in range(share)]
    taps = stencil_coefficients
    near_plane, partial = ends_call(me, far_plane, x, taps)
    near_halo = lax.ppermute(near_plane, "gx", near_pairs)
    inside_probs, sums, mass, maps = inside_call(
        x, taps, partition_affinity_matrix, softness_mapping_matrix[None], n.bit_length() - 1
    )
    near_probs, sums, mass = edge_call(
        False, me, near_halo, taps, maps, partial, sums, mass, 2 * owners
    )
    by_slice, send, sums, mass, hid = edge_call(
        True, me, far_halo, taps, maps, partial, sums, mass, 2 * owners
    )

    received = lax.ppermute(send, "gx", near_pairs)
    keep, far_probs = keep_call(me, by_slice, hid, sums, mass, send.shape, GROUP * depth)
    parts = merge_call(keep, received)
    parts = lax.all_to_all(parts, "gx", 0, 0, axis_index_groups=groups)
    if share > 1:
        sharers = [[2 * (share * j + s) + h for s in range(share)]
                   for h in range(2) for j in range(owners)]
        parts = lax.psum(parts, "gx", axis_index_groups=sharers)
    own_out, mapped = owner_call(
        parts, layernorm_multiplier[None],
        content_mapping_matrix, widening_matrix, narrowing_matrix, final_mapping_matrix,
    )
    if share > 1:
        place = lax.rem(me[0] // 2, share) * (slices // n)
        own_out = lax.dynamic_slice_in_dim(own_out, place, slices // n)
    mapped = lax.all_to_all(mapped, "gx", 0, 0, axis_index_groups=groups).reshape(slices // 2, channels)
    other = lax.ppermute(mapped, "gx", near_pairs)
    planes_of_cells = x.reshape(planes, height * depth, channels)
    ahead = ahead_call(me, planes_of_cells, inside_probs, near_probs, mapped)
    updated = update_call(
        me, planes_of_cells, ahead, inside_probs, near_probs, far_probs, mapped, other
    )
    return updated.reshape(x.shape), own_out


def solution(mesh):
    return jax.shard_map(
        per_device,
        mesh=mesh,
        in_specs=(P(("grp", "gx"), None, None, None), P(), P(), P(), P(), P(), P(), P(), P()),
        out_specs=(P(("grp", "gx"), None, None, None), P(("grp", "gx"), None)),
        check_vma=False,
    )
```

profile of v0, /device:TPU:0, one launch (start us, length us, event | category | flops | bytes accessed | tf_op | source)
XLA Modules:
  0.0 68.7 jit_solution(12629105270820737475)
XLA Ops:
  0.6 1.3 %constant_dynamic-slice_fusion._ = bf16[1,32,32,512]{3,2,1,0:T(8,128)(2,1)S(1)} fusion(bf16[4,32,32,512]{3,2,1,0:T(8,128)(2,1)} %x_ref.3, s32[]{:T(128)S(6)} %select_n.3), kind=kLoop, calls=%fused_computation | loop fusion | bytes 2097156 | tf_op jit(solution)/shard_map/dynamic_slice | solution.py:537
  1.9 0.7 %collective-permute-start.1 = (bf16[1,32,32,512]{3,2,1,0:T(8,128)(2,1)S(1)}, bf16[1,32,32,512]{3,2,1,0:T(8,128)(2,1)S(1)}, u32[]{:S(2)}, u32[]{:S(2)}) collective-permute-start(bf16[1,32,32,512]{3,2,1,0:T(8,128)(2,1)S(1)} %constant_dynamic-slice_fusion._), channel_id=1, source_target_pairs={{1,2},{2,1},{3,4},{4,3},{5,6},{6,5},{7,8},{8,7},{9,10},{10,9},{11,... | collective-permute-start | bytes 3145736 | tf_op jit(solution)/shard_map/ppermute | solution.py:538
  2.7 0.0 copy-start
  2.7 2.2 %copy-done = bf16[4,32,32,512]{3,2,1,0:T(8,128)(2,1)S(1)} copy-done((bf16[4,32,32,512]{3,2,1,0:T(8,128)(2,1)S(1)}, bf16[4,32,32,512]{3,2,1,0:T(8,128)(2,1)}, u32[]{:S(2)}) %copy-start) | copy-done | bytes 4194328
  4.9 0.8 %copy-done.8 = f32[27,512]{1,0:T(8,128)S(1)} copy-done((f32[27,512]{1,0:T(8,128)S(1)}, f32[27,512]{1,0:T(8,128)}, u32[]{:S(2)}) %copy-start.8) | copy-done | bytes 55320
  5.7 4.0 %ends.1 = (bf16[1,32,32,512]{3,2,1,0:T(8,128)(2,1)S(1)}, bf16[2,1024,512]{2,1,0:T(8,128)(2,1)S(1)}) custom-call(s32[1]{0:T(128)} %bitcast.me_ref, bf16[1,32,32,512]{3,2,1,0:T(8,128)(2,1)S(1)} %constant_dynamic-slice_fusion._, bf16[4,32,32,512]{3,2,1,0:T(8,128)(2,1)S(1)} %copy-done, f32[27,512]{1,0:T(8,128)S(1)} %copy-done.8), custom_call_target="tpu_custom_call" | custom-call | flops 6291456000 | bytes 4194304 | tf_op jit(solution)/shard_map/ends/pallas_call | solution.py:139
  9.7 4.3 %collective-permute-start = (bf16[1,32,32,512]{3,2,1,0:T(8,128)(2,1)S(1)}, bf16[1,32,32,512]{3,2,1,0:T(8,128)(2,1)S(1)}, u32[]{:S(2)}, u32[]{:S(2)}) collective-permute-start(bf16[1,32,32,512]{3,2,1,0:T(8,128)(2,1)S(1)} %get-tuple-element.21), channel_id=1, source_target_pairs={{0,1},{1,0},{2,3},{3,2},{4,5},{5,4},{6,7},{7,6},{8,9},{9,8},{10,11... | collective-permute-start | bytes 3145736 | tf_op jit(solution)/shard_map/ppermute | solution.py:545
  14.0 10.8 %inside.1 = (bf16[2,1024,512]{2,1,0:T(8,128)(2,1)S(1)}, f32[512,512]{1,0:T(8,128)S(1)}, f32[512,128]{1,0:T(8,128)S(1)}, bf16[528,512]{1,0:T(8,128)(2,1)S(1)}) custom-call(bf16[4,32,32,512]{3,2,1,0:T(8,128)(2,1)S(1)} %copy-done, f32[27,512]{1,0:T(8,128)S(1)} %copy-done.9, bf16[512,512]{1,0:T(8,128)(2,1)S(1)} %copy-done.7, f32[1,512]{1,0:T(1,128)S(1)} %bitcast.12), custom_call_target="tpu_custom_call" | custom-call | flops 14680064000 | bytes 4194304 | tf_op jit(solution)/shard_map/inside/pallas_call | solution.py:226
  24.8 3.1 %near.1 = (bf16[1,1024,512]{2,1,0:T(8,128)(2,1)S(1)}, f32[512,512]{1,0:T(8,128)S(1)}, f32[512,128]{1,0:T(8,128)S(1)}) custom-call(s32[1]{0:T(128)} %bitcast.me_ref, bf16[1,32,32,512]{3,2,1,0:T(8,128)(2,1)S(1)} %collective-permute-done.halo_ref, bf16[2,1024,512]{2,1,0:T(8,128)(2,1)S(1)} %get-tuple-element.22.partial_ref, f32[27,512]{1,0:T(8,128)S(1)} %copy-done.9, ...), custom_call_target="tpu_custom_call" | custom-call | flops 8388608000 | bytes 2097152 | tf_op jit(solution)/shard_map/near/pallas_call | solution.py:350
  27.9 3.6 %far.1 = (bf16[512,1024]{1,0:T(8,128)(2,1)S(1)}, bf16[8,136,128]{2,1,0:T(8,128)(2,1)S(1)}, f32[512,512]{1,0:T(8,128)S(1)}, f32[512,128]{1,0:T(8,128)S(1)}, bf16[1024,512]{1,0:T(8,128)(2,1)S(1)}) custom-call(s32[1]{0:T(128)} %bitcast.me_ref, bf16[1,32,32,512]{3,2,1,0:T(8,128)(2,1)S(1)} %collective-permute-done.1.halo_ref, ...), custom_call_target="tpu_custom_call" | custom-call | flops 8388608000 | bytes 2097152 | tf_op jit(solution)/shard_map/far/pallas_call | solution.py:350
  31.5 0.0 copy-start.2
  31.5 0.0 copy-start.3
  31.5 0.0 copy-start.4
  31.6 0.0 copy-start.5
  31.6 2.0 %collective-permute-start.2 = (bf16[8,136,128]{2,1,0:T(8,128)(2,1)S(1)}, bf16[8,136,128]{2,1,0:T(8,128)(2,1)S(1)}, u32[]{:S(2)}, u32[]{:S(2)}) collective-permute-start(bf16[8,136,128]{2,1,0:T(8,128)(2,1)S(1)} %get-tuple-element.34), channel_id=1, source_target_pairs={{0,1},{1,0},{2,3},{3,2},{4,5},{5,4},{6,7},{7,6},{8,9},{9,8},{10,11... | collective-permute-start | bytes 835592 | tf_op jit(solution)/shard_map/ppermute | solution.py:556
  33.6 0.5 keep.1
  34.1 0.7 collective-permute-done.2.other_ref
  34.8 0.1 merge.1
  34.8 16.2 %all_to_all.10.parts_ref = bf16[8,136,128]{2,1,0:T(8,128)(2,1)S(1)} all-to-all(bf16[8,136,128]{2,1,0:T(8,128)(2,1)S(1)} %merge.1), channel_id=1, replica_groups={{0,2,4,6,8,10,12,14},{1,3,5,7,9,11,13,15},{16,18,20,22,24,26,28,30},{17..., dimensions={0} | all-to-all | bytes 557056 | tf_op jit(solution)/shard_map/all_to_all | solution.py:559
  51.1 1.6 %owner.1 = (bf16[32,512]{1,0:T(8,128)(2,1)}, bf16[8,32,512]{2,1,0:T(8,128)(2,1)S(1)}) custom-call(bf16[8,136,128]{2,1,0:T(8,128)(2,1)S(1)} %all_to_all.10.parts_ref, f32[1,512]{1,0:T(1,128)S(1)} %bitcast.11, bf16[512,512]{1,0:T(8,128)(2,1)S(1)} %copy-done.4, bf16[512,1024]{1,0:T(8,128)(2,1)S(1)} %copy-done.2, bf16[1024,512]{1,0:T(8,128)(2,1)S(1)} %copy-done.3, ...), custom_call_target="tpu_custom_call" | custom-call | tf_op jit(solution)/shard_map/owner/pallas_call | solution.py:413
  52.7 11.4 %all_to_all.11 = bf16[8,32,512]{2,1,0:T(8,128)(2,1)S(1)} all-to-all(bf16[8,32,512]{2,1,0:T(8,128)(2,1)S(1)} %get-tuple-element.35), channel_id=1, replica_groups={{0,2,4,6,8,10,12,14},{1,3,5,7,9,11,13,15},{16,18,20,22,24,26,28,30},{17..., dimensions={0} | all-to-all | bytes 524288 | tf_op jit(solution)/shard_map/all_to_all | solution.py:571
  64.0 1.3 %ahead.1.ahead_ref = f32[3,1024,512]{2,1,0:T(8,128)S(1)} custom-call(s32[1]{0:T(128)} %bitcast.me_ref, bf16[4,1024,512]{2,1,0:T(8,128)(2,1)S(1)} %bitcast.6, bf16[2,1024,512]{2,1,0:T(8,128)(2,1)S(1)} %get-tuple-element.20.inside_ref, bf16[1,1024,512]{2,1,0:T(8,128)(2,1)S(1)} %get-tuple-element.26.near_ref, bf16[256,512]{1,0:T(8,128)(2,1)S(1)} %bitcast.9), custom_call_target="tpu_custom_call" | custom-call | flops 1073741824 | bytes 8388608 | tf_op jit(solution)/shard_map/ahead/pallas_call | solution.py:444
  65.3 0.2 collective-permute-done.3.other_ref
  65.6 3.1 %update.1 = bf16[4,1024,512]{2,1,0:T(8,128)(2,1)} custom-call(s32[1]{0:T(128)} %bitcast.me_ref, bf16[4,1024,512]{2,1,0:T(8,128)(2,1)S(1)} %bitcast.7, f32[3,1024,512]{2,1,0:T(8,128)S(1)} %ahead.1.ahead_ref, bf16[2,1024,512]{2,1,0:T(8,128)(2,1)S(1)} %get-tuple-element.20.inside_ref, bf16[1,1024,512]{2,1,0:T(8,128)(2,1)S(1)} %get-tuple-element.26.near_ref, ...), custom_call_target="tpu_custom_call" | custom-call | tf_op jit(solution)/shard_map/update/pallas_call | solution.py:504
  (18 shorter events, 0.0 us)
Async XLA Ops:
  1.9 26.0 %collective-permute-start.1 = (bf16[1,32,32,512]{3,2,1,0:T(8,128)(2,1)S(1)}, bf16[1,32,32,512]{3,2,1,0:T(8,128)(2,1)S(1)}, u32[]{:S(2)}, u32[]{:S(2)}) collective-permute-start(bf16[1,32,32,512]{3,2,1,0:T(8,128)(2,1)S(1)} %constant_dynamic-slice_fusion._), channel_id=1, source_target_pairs={{1,2},{2,1},{3,4},{4,3},{5,6},{6,5},{7,8},{8,7},{9,10},{10,9},{11,... | collective-permute-start | bytes 3145736 | tf_op jit(solution)/shard_map/ppermute | solution.py:538
  2.7 2.2 %copy-start = (bf16[4,32,32,512]{3,2,1,0:T(8,128)(2,1)S(1)}, bf16[4,32,32,512]{3,2,1,0:T(8,128)(2,1)}, u32[]{:S(2)}) copy-start(bf16[4,32,32,512]{3,2,1,0:T(8,128)(2,1)} %x_ref.3) | copy-start | bytes 12582916
  4.9 0.8 %copy-start.8 = (f32[27,512]{1,0:T(8,128)S(1)}, f32[27,512]{1,0:T(8,128)}, u32[]{:S(2)}) copy-start(f32[27,512]{1,0:T(8,128)} %k_ref.7) | copy-start | bytes 165892
  5.7 8.3 %copy-start.7 = (bf16[512,512]{1,0:T(8,128)(2,1)S(1)}, bf16[512,512]{1,0:T(8,128)(2,1)}, u32[]{:S(2)}) copy-start(bf16[512,512]{1,0:T(8,128)(2,1)} %affinity_ref.1) | copy-start | bytes 1572868
  5.7 8.3 %copy-start.9 = (f32[27,512]{1,0:T(8,128)S(1)}, f32[27,512]{1,0:T(8,128)}, u32[]{:S(2)}) copy-start(f32[27,512]{1,0:T(8,128)} %k_ref.7) | copy-start | bytes 165892
  5.7 8.3 %copy-start.10 = (f32[512]{0:T(512)S(1)}, f32[512]{0:T(512)}, u32[]{:S(2)}) copy-start(f32[512]{0:T(512)} %param.12) | copy-start | bytes 6148
  9.7 15.1 %collective-permute-start = (bf16[1,32,32,512]{3,2,1,0:T(8,128)(2,1)S(1)}, bf16[1,32,32,512]{3,2,1,0:T(8,128)(2,1)S(1)}, u32[]{:S(2)}, u32[]{:S(2)}) collective-permute-start(bf16[1,32,32,512]{3,2,1,0:T(8,128)(2,1)S(1)} %get-tuple-element.21), channel_id=1, source_target_pairs={{0,1},{1,0},{2,3},{3,2},{4,5},{5,4},{6,7},{7,6},{8,9},{9,8},{10,11... | collective-permute-start | bytes 3145736 | tf_op jit(solution)/shard_map/ppermute | solution.py:545
  31.5 19.5 %copy-start.2 = (bf16[512,1024]{1,0:T(8,128)(2,1)S(1)}, bf16[512,1024]{1,0:T(8,128)(2,1)}, u32[]{:S(2)}) copy-start(bf16[512,1024]{1,0:T(8,128)(2,1)} %widening_ref.1) | copy-start | bytes 3145732
  31.5 19.5 %copy-start.3 = (bf16[1024,512]{1,0:T(8,128)(2,1)S(1)}, bf16[1024,512]{1,0:T(8,128)(2,1)}, u32[]{:S(2)}) copy-start(bf16[1024,512]{1,0:T(8,128)(2,1)} %narrowing_ref.1) | copy-start | bytes 3145732
  31.5 19.5 %copy-start.4 = (bf16[512,512]{1,0:T(8,128)(2,1)S(1)}, bf16[512,512]{1,0:T(8,128)(2,1)}, u32[]{:S(2)}) copy-start(bf16[512,512]{1,0:T(8,128)(2,1)} %content_ref.1) | copy-start | bytes 1572868
  31.6 19.5 %copy-start.5 = (bf16[512,512]{1,0:T(8,128)(2,1)S(1)}, bf16[512,512]{1,0:T(8,128)(2,1)}, u32[]{:S(2)}) copy-start(bf16[512,512]{1,0:T(8,128)(2,1)} %final_ref.1) | copy-start | bytes 1572868
  31.6 19.5 %copy-start.6 = (f32[512]{0:T(512)S(1)}, f32[512]{0:T(512)}, u32[]{:S(2)}) copy-start(f32[512]{0:T(512)} %param.14) | copy-start | bytes 6148
  31.6 3.2 %collective-permute-start.2 = (bf16[8,136,128]{2,1,0:T(8,128)(2,1)S(1)}, bf16[8,136,128]{2,1,0:T(8,128)(2,1)S(1)}, u32[]{:S(2)}, u32[]{:S(2)}) collective-permute-start(bf16[8,136,128]{2,1,0:T(8,128)(2,1)S(1)} %get-tuple-element.34), channel_id=1, source_target_pairs={{0,1},{1,0},{2,3},{3,2},{4,5},{5,4},{6,7},{7,6},{8,9},{9,8},{10,11... | collective-permute-start | bytes 835592 | tf_op jit(solution)/shard_map/ppermute | solution.py:556
  33.6 30.5 %copy-start.1 = (bf16[4,32,32,512]{3,2,1,0:T(8,128)(2,1)S(1)}, bf16[4,32,32,512]{3,2,1,0:T(8,128)(2,1)}, u32[]{:S(2)}) copy-start(bf16[4,32,32,512]{3,2,1,0:T(8,128)(2,1)} %x_ref.3) | copy-start | bytes 12582916
  64.0 1.5 %collective-permute-start.3 = (bf16[256,512]{1,0:T(8,128)(2,1)S(1)}, bf16[256,512]{1,0:T(8,128)(2,1)S(1)}, u32[]{:S(2)}, u32[]{:S(2)}) collective-permute-start(bf16[256,512]{1,0:T(8,128)(2,1)S(1)} %bitcast.8), channel_id=1, source_target_pairs={{0,1},{1,0},{2,3},{3,2},{4,5},{5,4},{6,7},{7,6},{8,9},{9,8},{10,11... | collective-permute-start | bytes 786440 | tf_op jit(solution)/shard_map/ppermute | solution.py:572
where the time goes:
time: 69 us; the launch traced here: 68.7 us
  Pallas kernels  28 us (41%)
  blocking collectives  27.6 us (40%)
  starting transfers between devices  7.01 us (10%)
  local copies, waits for them, and re-layouts  4.37 us (6%)
  waiting for transfers between devices  0.91 us (1%)
  between operations  0.78 us (1%)
    all_to_all x1, blocking collectives, per_device(): parts = lax.all_to_all(parts, 'gx', 0, 0, axis_index_groups=groups)  16.2 us
    all_to_all x1, blocking collectives, per_device(): lax.all_to_all(mapped, 'gx', 0, 0, axis_index_groups=groups)  11.4 us
    pallas_call x1, Pallas kernels, inside_call(): pl.pallas_call(functools.partial(inside_kernel, bits), in_specs=[VMEM] *...  10.8 us
    pallas_call x2, Pallas kernels, edge_call(): pl.pallas_call(functools.partial(edge_kernel, is_far), in_specs=[SMEM] +...  6.67 us
    ppermute x1, starting transfers between devices, per_device(): near_halo = lax.ppermute(near_plane, 'gx', near_pairs)  4.3 us
    pallas_call x1, Pallas kernels, ends_call(): pl.pallas_call(ends_kernel, in_specs=[SMEM, pl.BlockSpec(memory_space=pl....  3.99 us
    pallas_call x1, Pallas kernels, update_call(): pl.pallas_call(update_kernel, in_specs=[SMEM] + [VMEM] * 7, out_specs=HBM...  3.09 us
    unnamed x22, local copies, waits for them, and re-layouts  3.07 us
  transfers between devices with their start and end apart: 4, of which 2 were waited for; matrix products, arithmetic and copies ran while one was open for 0% of the time, Pallas kernels for 29%

commit v1 on v0

--- a/solution.py
+++ b/solution.py
@@ -82,23 +82,33 @@
     return lax.dot_general(a, b, (((1,), (1,)), ((), ())), preferred_element_type=F32)
 
 
-def assign(hid, map_ref, mass_ref):
+def assign_steps(hid, map_ref, mass_ref, result):
     cells = hid.shape[0]
     slices = map_ref.shape[0] - TILE
     raw = nt_dot(map_ref[...], hid)
+    yield
     soft = raw[slices : slices + 8]
     temperature = 0.25 + jnp.maximum(soft, 0.0) + jnp.log(1.0 + jnp.exp(-jnp.abs(soft)))
     scale = (1.0 / math.log(2.0)) / temperature
     raw = raw[:slices].reshape(slices // 8, 8, cells)
     top = jnp.max(jnp.max(raw, axis=0), axis=0, keepdims=True)
+    yield
     powers = jnp.exp2((raw - top[None]) * scale[None])
     total = jnp.sum(jnp.sum(powers, axis=0), axis=0, keepdims=True)
+    yield
     probs = (powers * (1.0 / total)[None]).reshape(slices, cells)
     mass = probs[:, :LANES]
     for start in range(LANES, cells, LANES):
         mass = mass + probs[:, start : start + LANES]
     mass_ref[...] += mass
-    return probs.astype(BF16)
+    result.append(probs.astype(BF16))
+
+
+def assign(hid, map_ref, mass_ref):
+    result = []
+    for _ in assign_steps(hid, map_ref, mass_ref, result):
+        pass
+    return result[0]
 
 
 def ends_kernel(me_ref, _, x_ref, k_ref, near_ref, partial_ref, taps_ref):
@@ -262,22 +272,28 @@
     cells = GROUP * depth
     most = height * depth - cells
 
-    def conv(first):
-        for lanes in channel_blocks(channels):
-            for y in range(first, first + GROUP, 2):
+    def conv_steps(first):
+        for y in range(first, min(first + GROUP, height), 2):
+            for lanes in channel_blocks(channels):
                 rows = [halo_ref[0, y + b, :, lanes] if 0 <= y + b < height else None
                         for b in (-1, 0, 1, 2)]
                 ats = [slice((y + i) * depth, (y + i + 1) * depth) for i in range(2)]
                 known = [partial_ref[side, at, lanes] for at in ats]
                 for at, total in zip(ats, conv_rows([(0, rows)], taps_ref, lanes, 2, known)):
                     hid_ref[at, lanes] = gelu(total.astype(BF16))
-
-    conv(0)
+                yield
+
+    for _ in conv_steps(0):
+        pass
     for first in range(0, height, GROUP):
-        if first + GROUP < height:
-            conv(first + GROUP)
         group = slice(first * depth, first * depth + cells)
-        by_slice = assign(hid_ref[group], map_ref, mass_ref)
+        result, conv = [], conv_steps(first + GROUP)
+        for _ in assign_steps(hid_ref[group], map_ref, mass_ref, result):
+            next(conv, None)
+            next(conv, None)
+        for _ in conv:
+            pass
+        by_slice, = result
         if not is_far:
             probs_ref[0, group] = by_slice.T
         by_slice_ref[:, group] = by_slice

time: 69 us -> 69 us (level)
  no operation moved by 1% of the time
where the time goes in v1:
time: 69 us; the launch traced here: 68.7 us
  Pallas kernels  28 us (41%)
  blocking collectives  27.6 us (40%)
  starting transfers between devices  7.01 us (10%)
  local copies, waits for them, and re-layouts  4.37 us (6%)
  waiting for transfers between devices  0.91 us (1%)
  between operations  0.78 us (1%)
    all_to_all x1, blocking collectives, per_device(): parts = lax.all_to_all(parts, 'gx', 0, 0, axis_index_groups=groups)  16.2 us
    all_to_all x1, blocking collectives, per_device(): lax.all_to_all(mapped, 'gx', 0, 0, axis_index_groups=groups)  11.4 us
    pallas_call x1, Pallas kernels, inside_call(): pl.pallas_call(functools.partial(inside_kernel, bits), in_specs=[VMEM] *...  10.8 us
    pallas_call x2, Pallas kernels, edge_call(): pl.pallas_call(functools.partial(edge_kernel, is_far), in_specs=[SMEM] +...  6.67 us
    ppermute x1, starting transfers between devices, per_device(): near_halo = lax.ppermute(near_plane, 'gx', near_pairs)  4.3 us
    pallas_call x1, Pallas kernels, ends_call(): pl.pallas_call(ends_kernel, in_specs=[SMEM, pl.BlockSpec(memory_space=pl....  3.99 us
    pallas_call x1, Pallas kernels, update_call(): pl.pallas_call(update_kernel, in_specs=[SMEM] + [VMEM] * 7, out_specs=HBM...  3.09 us
    unnamed x22, local copies, waits for them, and re-layouts  3.07 us
  transfers between devices with their start and end apart: 4, of which 2 were waited for; matrix products, arithmetic and copies ran while one was open for 0% of the time, Pallas kernels for 29%

profile of v1, /device:TPU:0, one launch (start us, length us, event | category | flops | bytes accessed | tf_op | source)
XLA Modules:
  0.0 68.7 jit_solution(12629105270820737475)
XLA Ops:
  0.6 1.3 %constant_dynamic-slice_fusion._ = bf16[1,32,32,512]{3,2,1,0:T(8,128)(2,1)S(1)} fusion(bf16[4,32,32,512]{3,2,1,0:T(8,128)(2,1)} %x_ref.3, s32[]{:T(128)S(6)} %select_n.3), kind=kLoop, calls=%fused_computation | loop fusion | bytes 2097156 | tf_op jit(solution)/shard_map/dynamic_slice | solution.py:553
  1.9 0.7 %collective-permute-start.1 = (bf16[1,32,32,512]{3,2,1,0:T(8,128)(2,1)S(1)}, bf16[1,32,32,512]{3,2,1,0:T(8,128)(2,1)S(1)}, u32[]{:S(2)}, u32[]{:S(2)}) collective-permute-start(bf16[1,32,32,512]{3,2,1,0:T(8,128)(2,1)S(1)} %constant_dynamic-slice_fusion._), channel_id=1, source_target_pairs={{1,2},{2,1},{3,4},{4,3},{5,6},{6,5},{7,8},{8,7},{9,10},{10,9},{11,... | collective-permute-start | bytes 3145736 | tf_op jit(solution)/shard_map/ppermute | solution.py:554
  2.7 0.0 copy-start
  2.7 2.2 %copy-done = bf16[4,32,32,512]{3,2,1,0:T(8,128)(2,1)S(1)} copy-done((bf16[4,32,32,512]{3,2,1,0:T(8,128)(2,1)S(1)}, bf16[4,32,32,512]{3,2,1,0:T(8,128)(2,1)}, u32[]{:S(2)}) %copy-start) | copy-done | bytes 4194328
  4.9 0.8 %copy-done.8 = f32[27,512]{1,0:T(8,128)S(1)} copy-done((f32[27,512]{1,0:T(8,128)S(1)}, f32[27,512]{1,0:T(8,128)}, u32[]{:S(2)}) %copy-start.8) | copy-done | bytes 55320
  5.7 4.0 %ends.1 = (bf16[1,32,32,512]{3,2,1,0:T(8,128)(2,1)S(1)}, bf16[2,1024,512]{2,1,0:T(8,128)(2,1)S(1)}) custom-call(s32[1]{0:T(128)} %bitcast.me_ref, bf16[1,32,32,512]{3,2,1,0:T(8,128)(2,1)S(1)} %constant_dynamic-slice_fusion._, bf16[4,32,32,512]{3,2,1,0:T(8,128)(2,1)S(1)} %copy-done, f32[27,512]{1,0:T(8,128)S(1)} %copy-done.8), custom_call_target="tpu_custom_call" | custom-call | flops 6291456000 | bytes 4194304 | tf_op jit(solution)/shard_map/ends/pallas_call | solution.py:149
  9.7 4.3 %collective-permute-start = (bf16[1,32,32,512]{3,2,1,0:T(8,128)(2,1)S(1)}, bf16[1,32,32,512]{3,2,1,0:T(8,128)(2,1)S(1)}, u32[]{:S(2)}, u32[]{:S(2)}) collective-permute-start(bf16[1,32,32,512]{3,2,1,0:T(8,128)(2,1)S(1)} %get-tuple-element.21), channel_id=1, source_target_pairs={{0,1},{1,0},{2,3},{3,2},{4,5},{5,4},{6,7},{7,6},{8,9},{9,8},{10,11... | collective-permute-start | bytes 3145736 | tf_op jit(solution)/shard_map/ppermute | solution.py:561
  14.0 10.8 %inside.1 = (bf16[2,1024,512]{2,1,0:T(8,128)(2,1)S(1)}, f32[512,512]{1,0:T(8,128)S(1)}, f32[512,128]{1,0:T(8,128)S(1)}, bf16[528,512]{1,0:T(8,128)(2,1)S(1)}) custom-call(bf16[4,32,32,512]{3,2,1,0:T(8,128)(2,1)S(1)} %copy-done, f32[27,512]{1,0:T(8,128)S(1)} %copy-done.9, bf16[512,512]{1,0:T(8,128)(2,1)S(1)} %copy-done.7, f32[1,512]{1,0:T(1,128)S(1)} %bitcast.12), custom_call_target="tpu_custom_call" | custom-call | flops 14680064000 | bytes 4194304 | tf_op jit(solution)/shard_map/inside/pallas_call | solution.py:236
  24.8 3.1 %near.1 = (bf16[1,1024,512]{2,1,0:T(8,128)(2,1)S(1)}, f32[512,512]{1,0:T(8,128)S(1)}, f32[512,128]{1,0:T(8,128)S(1)}) custom-call(s32[1]{0:T(128)} %bitcast.me_ref, bf16[1,32,32,512]{3,2,1,0:T(8,128)(2,1)S(1)} %collective-permute-done.halo_ref, bf16[2,1024,512]{2,1,0:T(8,128)(2,1)S(1)} %get-tuple-element.22.partial_ref, f32[27,512]{1,0:T(8,128)S(1)} %copy-done.9, ...), custom_call_target="tpu_custom_call" | custom-call | flops 8388608000 | bytes 2097152 | tf_op jit(solution)/shard_map/near/pallas_call | solution.py:366
  27.9 3.6 %far.1 = (bf16[512,1024]{1,0:T(8,128)(2,1)S(1)}, bf16[8,136,128]{2,1,0:T(8,128)(2,1)S(1)}, f32[512,512]{1,0:T(8,128)S(1)}, f32[512,128]{1,0:T(8,128)S(1)}, bf16[1024,512]{1,0:T(8,128)(2,1)S(1)}) custom-call(s32[1]{0:T(128)} %bitcast.me_ref, bf16[1,32,32,512]{3,2,1,0:T(8,128)(2,1)S(1)} %collective-permute-done.1.halo_ref, ...), custom_call_target="tpu_custom_call" | custom-call | flops 8388608000 | bytes 2097152 | tf_op jit(solution)/shard_map/far/pallas_call | solution.py:366
  31.5 0.0 copy-start.2
  31.5 0.0 copy-start.3
  31.5 0.0 copy-start.4
  31.6 0.0 copy-start.5
  31.6 2.0 %collective-permute-start.2 = (bf16[8,136,128]{2,1,0:T(8,128)(2,1)S(1)}, bf16[8,136,128]{2,1,0:T(8,128)(2,1)S(1)}, u32[]{:S(2)}, u32[]{:S(2)}) collective-permute-start(bf16[8,136,128]{2,1,0:T(8,128)(2,1)S(1)} %get-tuple-element.34), channel_id=1, source_target_pairs={{0,1},{1,0},{2,3},{3,2},{4,5},{5,4},{6,7},{7,6},{8,9},{9,8},{10,11... | collective-permute-start | bytes 835592 | tf_op jit(solution)/shard_map/ppermute | solution.py:572
  33.6 0.5 keep.1
  34.1 0.7 collective-permute-done.2.other_ref
  34.8 0.1 merge.1
  34.8 16.2 %all_to_all.10.parts_ref = bf16[8,136,128]{2,1,0:T(8,128)(2,1)S(1)} all-to-all(bf16[8,136,128]{2,1,0:T(8,128)(2,1)S(1)} %merge.1), channel_id=1, replica_groups={{0,2,4,6,8,10,12,14},{1,3,5,7,9,11,13,15},{16,18,20,22,24,26,28,30},{17..., dimensions={0} | all-to-all | bytes 557056 | tf_op jit(solution)/shard_map/all_to_all | solution.py:575
  51.1 1.6 %owner.1 = (bf16[32,512]{1,0:T(8,128)(2,1)}, bf16[8,32,512]{2,1,0:T(8,128)(2,1)S(1)}) custom-call(bf16[8,136,128]{2,1,0:T(8,128)(2,1)S(1)} %all_to_all.10.parts_ref, f32[1,512]{1,0:T(1,128)S(1)} %bitcast.11, bf16[512,512]{1,0:T(8,128)(2,1)S(1)} %copy-done.4, bf16[512,1024]{1,0:T(8,128)(2,1)S(1)} %copy-done.2, bf16[1024,512]{1,0:T(8,128)(2,1)S(1)} %copy-done.3, ...), custom_call_target="tpu_custom_call" | custom-call | tf_op jit(solution)/shard_map/owner/pallas_call | solution.py:429
  52.7 11.4 %all_to_all.11 = bf16[8,32,512]{2,1,0:T(8,128)(2,1)S(1)} all-to-all(bf16[8,32,512]{2,1,0:T(8,128)(2,1)S(1)} %get-tuple-element.35), channel_id=1, replica_groups={{0,2,4,6,8,10,12,14},{1,3,5,7,9,11,13,15},{16,18,20,22,24,26,28,30},{17..., dimensions={0} | all-to-all | bytes 524288 | tf_op jit(solution)/shard_map/all_to_all | solution.py:587
  64.0 1.3 %ahead.1.ahead_ref = f32[3,1024,512]{2,1,0:T(8,128)S(1)} custom-call(s32[1]{0:T(128)} %bitcast.me_ref, bf16[4,1024,512]{2,1,0:T(8,128)(2,1)S(1)} %bitcast.6, bf16[2,1024,512]{2,1,0:T(8,128)(2,1)S(1)} %get-tuple-element.20.inside_ref, bf16[1,1024,512]{2,1,0:T(8,128)(2,1)S(1)} %get-tuple-element.26.near_ref, bf16[256,512]{1,0:T(8,128)(2,1)S(1)} %bitcast.9), custom_call_target="tpu_custom_call" | custom-call | flops 1073741824 | bytes 8388608 | tf_op jit(solution)/shard_map/ahead/pallas_call | solution.py:460
  65.3 0.2 collective-permute-done.3.other_ref
  65.6 3.1 %update.1 = bf16[4,1024,512]{2,1,0:T(8,128)(2,1)} custom-call(s32[1]{0:T(128)} %bitcast.me_ref, bf16[4,1024,512]{2,1,0:T(8,128)(2,1)S(1)} %bitcast.7, f32[3,1024,512]{2,1,0:T(8,128)S(1)} %ahead.1.ahead_ref, bf16[2,1024,512]{2,1,0:T(8,128)(2,1)S(1)} %get-tuple-element.20.inside_ref, bf16[1,1024,512]{2,1,0:T(8,128)(2,1)S(1)} %get-tuple-element.26.near_ref, ...), custom_call_target="tpu_custom_call" | custom-call | tf_op jit(solution)/shard_map/update/pallas_call | solution.py:520
  (18 shorter events, 0.0 us)
Async XLA Ops:
  1.9 26.0 %collective-permute-start.1 = (bf16[1,32,32,512]{3,2,1,0:T(8,128)(2,1)S(1)}, bf16[1,32,32,512]{3,2,1,0:T(8,128)(2,1)S(1)}, u32[]{:S(2)}, u32[]{:S(2)}) collective-permute-start(bf16[1,32,32,512]{3,2,1,0:T(8,128)(2,1)S(1)} %constant_dynamic-slice_fusion._), channel_id=1, source_target_pairs={{1,2},{2,1},{3,4},{4,3},{5,6},{6,5},{7,8},{8,7},{9,10},{10,9},{11,... | collective-permute-start | bytes 3145736 | tf_op jit(solution)/shard_map/ppermute | solution.py:554
  2.7 2.2 %copy-start = (bf16[4,32,32,512]{3,2,1,0:T(8,128)(2,1)S(1)}, bf16[4,32,32,512]{3,2,1,0:T(8,128)(2,1)}, u32[]{:S(2)}) copy-start(bf16[4,32,32,512]{3,2,1,0:T(8,128)(2,1)} %x_ref.3) | copy-start | bytes 12582916
  4.9 0.8 %copy-start.8 = (f32[27,512]{1,0:T(8,128)S(1)}, f32[27,512]{1,0:T(8,128)}, u32[]{:S(2)}) copy-start(f32[27,512]{1,0:T(8,128)} %k_ref.7) | copy-start | bytes 165892
  5.7 8.3 %copy-start.7 = (bf16[512,512]{1,0:T(8,128)(2,1)S(1)}, bf16[512,512]{1,0:T(8,128)(2,1)}, u32[]{:S(2)}) copy-start(bf16[512,512]{1,0:T(8,128)(2,1)} %affinity_ref.1) | copy-start | bytes 1572868
  5.7 8.3 %copy-start.9 = (f32[27,512]{1,0:T(8,128)S(1)}, f32[27,512]{1,0:T(8,128)}, u32[]{:S(2)}) copy-start(f32[27,512]{1,0:T(8,128)} %k_ref.7) | copy-start | bytes 165892
  5.7 8.3 %copy-start.10 = (f32[512]{0:T(512)S(1)}, f32[512]{0:T(512)}, u32[]{:S(2)}) copy-start(f32[512]{0:T(512)} %param.12) | copy-start | bytes 6148
  9.7 15.1 %collective-permute-start = (bf16[1,32,32,512]{3,2,1,0:T(8,128)(2,1)S(1)}, bf16[1,32,32,512]{3,2,1,0:T(8,128)(2,1)S(1)}, u32[]{:S(2)}, u32[]{:S(2)}) collective-permute-start(bf16[1,32,32,512]{3,2,1,0:T(8,128)(2,1)S(1)} %get-tuple-element.21), channel_id=1, source_target_pairs={{0,1},{1,0},{2,3},{3,2},{4,5},{5,4},{6,7},{7,6},{8,9},{9,8},{10,11... | collective-permute-start | bytes 3145736 | tf_op jit(solution)/shard_map/ppermute | solution.py:561
  31.5 19.5 %copy-start.2 = (bf16[512,1024]{1,0:T(8,128)(2,1)S(1)}, bf16[512,1024]{1,0:T(8,128)(2,1)}, u32[]{:S(2)}) copy-start(bf16[512,1024]{1,0:T(8,128)(2,1)} %widening_ref.1) | copy-start | bytes 3145732
  31.5 19.5 %copy-start.3 = (bf16[1024,512]{1,0:T(8,128)(2,1)S(1)}, bf16[1024,512]{1,0:T(8,128)(2,1)}, u32[]{:S(2)}) copy-start(bf16[1024,512]{1,0:T(8,128)(2,1)} %narrowing_ref.1) | copy-start | bytes 3145732
  31.5 19.5 %copy-start.4 = (bf16[512,512]{1,0:T(8,128)(2,1)S(1)}, bf16[512,512]{1,0:T(8,128)(2,1)}, u32[]{:S(2)}) copy-start(bf16[512,512]{1,0:T(8,128)(2,1)} %content_ref.1) | copy-start | bytes 1572868
  31.6 19.5 %copy-start.5 = (bf16[512,512]{1,0:T(8,128)(2,1)S(1)}, bf16[512,512]{1,0:T(8,128)(2,1)}, u32[]{:S(2)}) copy-start(bf16[512,512]{1,0:T(8,128)(2,1)} %final_ref.1) | copy-start | bytes 1572868
  31.6 19.5 %copy-start.6 = (f32[512]{0:T(512)S(1)}, f32[512]{0:T(512)}, u32[]{:S(2)}) copy-start(f32[512]{0:T(512)} %param.14) | copy-start | bytes 6148
  31.6 3.2 %collective-permute-start.2 = (bf16[8,136,128]{2,1,0:T(8,128)(2,1)S(1)}, bf16[8,136,128]{2,1,0:T(8,128)(2,1)S(1)}, u32[]{:S(2)}, u32[]{:S(2)}) collective-permute-start(bf16[8,136,128]{2,1,0:T(8,128)(2,1)S(1)} %get-tuple-element.34), channel_id=1, source_target_pairs={{0,1},{1,0},{2,3},{3,2},{4,5},{5,4},{6,7},{7,6},{8,9},{9,8},{10,11... | collective-permute-start | bytes 835592 | tf_op jit(solution)/shard_map/ppermute | solution.py:572
  33.6 30.5 %copy-start.1 = (bf16[4,32,32,512]{3,2,1,0:T(8,128)(2,1)S(1)}, bf16[4,32,32,512]{3,2,1,0:T(8,128)(2,1)}, u32[]{:S(2)}) copy-start(bf16[4,32,32,512]{3,2,1,0:T(8,128)(2,1)} %x_ref.3) | copy-start | bytes 12582916
  64.0 1.5 %collective-permute-start.3 = (bf16[256,512]{1,0:T(8,128)(2,1)S(1)}, bf16[256,512]{1,0:T(8,128)(2,1)S(1)}, u32[]{:S(2)}, u32[]{:S(2)}) collective-permute-start(bf16[256,512]{1,0:T(8,128)(2,1)S(1)} %bitcast.8), channel_id=1, source_target_pairs={{0,1},{1,0},{2,3},{3,2},{4,5},{5,4},{6,7},{7,6},{8,9},{9,8},{10,11... | collective-permute-start | bytes 786440 | tf_op jit(solution)/shard_map/ppermute | solution.py:588

commit v2 on v1

--- a/solution.py
+++ b/solution.py
@@ -478,41 +478,35 @@
     mapped_ref[mine] = own_ref[...]
     mapped_ref[others] = other_ref[...]
 
-    pieces = 2
-    rows = cells // pieces
     near, far = (planes - 1) * (1 - odd), (planes - 1) * odd
 
-    def store(plane, piece):
-        at = pl.ds(pl.multiple_of(piece * rows, rows), rows)
-        return pltpu.make_async_copy(
-            done_ref.at[plane, at], out_ref.at[plane, at], sem.at[plane * pieces + piece]
-        )
+    def store(plane, at, sem_ref):
+        return pltpu.make_async_copy(done_ref.at[plane, at], out_ref.at[plane, at], sem_ref)
+
+    def whole(plane):
+        return store(plane, pl.ds(0, cells), sem.at[plane])
 
     def step(i, carry):
-        part, piece = i // pieces, lax.rem(i, pieces)
-        at = pl.ds(pl.multiple_of(piece * rows, rows), rows)
-        total = ahead_ref[part, at, :] + dot(inside_ref[part, at, others], other_ref[...])
-        done_ref[part + 1, at, :] = total.astype(BF16)
-        store(part + 1, piece).start()
+        total = ahead_ref[i] + dot(inside_ref[i, :, others], other_ref[...])
+        done_ref[i + 1] = total.astype(BF16)
+        whole(i + 1).start()
         return carry
 
-    lax.fori_loop(0, (planes - 2) * pieces, step, 0)
-    for piece in range(pieces):
-        at = pl.ds(piece * rows, rows)
-        total = ahead_ref[planes - 2, at, :] + dot(near_ref[0, at, others], other_ref[...])
-        done_ref[near, at, :] = total.astype(BF16)
-        store(near, piece).start()
-    for piece in range(pieces):
-        at = pl.ds(piece * rows, rows)
+    lax.fori_loop(0, planes - 2, step, 0)
+    total = ahead_ref[planes - 2] + dot(near_ref[0, :, others], other_ref[...])
+    done_ref[near] = total.astype(BF16)
+    whole(near).start()
+    parts = [pl.ds(0, cells // 2), pl.ds(cells // 2, cells // 2)]
+    lasts = [store(far, at, sem.at[planes + i]) for i, at in enumerate(parts)]
+    for at, last in zip(parts, lasts):
         change = dot(far_ref[0, at], mapped_ref[...])
         done_ref[far, at, :] = (x_ref[far, at, :].astype(F32) + change).astype(BF16)
-        store(far, piece).start()
-
-    def finish(i, carry):
-        store(i // pieces, lax.rem(i, pieces)).wait()
-        return carry
-
-    lax.fori_loop(0, planes * pieces, finish, 0)
+        last.start()
+    whole(near).wait()
+    for i in range(planes - 2):
+        whole(i + 1).wait()
+    for last in lasts:
+        last.wait()
 
 
 def update_call(me, x, ahead, inside, near, far, own, other):
@@ -525,7 +519,7 @@
         scratch_shapes=[
             pltpu.VMEM(x.shape, BF16),
             pltpu.VMEM((2 * own.shape[0], channels), BF16),
-            pltpu.SemaphoreType.DMA((2 * planes,)),
+            pltpu.SemaphoreType.DMA((planes + 2,)),
         ],
         compiler_params=pltpu.CompilerParams(vmem_limit_bytes=LIMIT),
         name="update",

time: 69 us -> 68.8 us (level)
  no operation moved by 1% of the time
where the time goes in v2:
time: 68.8 us; the launch traced here: 68.5 us
  Pallas kernels  27.7 us (40%)
  blocking collectives  27.6 us (40%)
  starting transfers between devices  7 us (10%)
  local copies, waits for them, and re-layouts  4.37 us (6%)
  between operations  0.93 us (1%)
  waiting for transfers between devices  0.91 us (1%)
    all_to_all x1, blocking collectives, per_device(): parts = lax.all_to_all(parts, 'gx', 0, 0, axis_index_groups=groups)  16.2 us
    all_to_all x1, blocking collectives, per_device(): lax.all_to_all(mapped, 'gx', 0, 0, axis_index_groups=groups)  11.4 us
    pallas_call x1, Pallas kernels, inside_call(): pl.pallas_call(functools.partial(inside_kernel, bits), in_specs=[VMEM] *...  10.8 us
    pallas_call x2, Pallas kernels, edge_call(): pl.pallas_call(functools.partial(edge_kernel, is_far), in_specs=[SMEM] +...  6.69 us
    ppermute x1, starting transfers between devices, per_device(): near_halo = lax.ppermute(near_plane, 'gx', near_pairs)  4.3 us
    pallas_call x1, Pallas kernels, ends_call(): pl.pallas_call(ends_kernel, in_specs=[SMEM, pl.BlockSpec(memory_space=pl....  3.99 us
    unnamed x22, local copies, waits for them, and re-layouts  3.07 us
    pallas_call x1, Pallas kernels, update_call(): pl.pallas_call(update_kernel, in_specs=[SMEM] + [VMEM] * 7, out_specs=HBM...  2.74 us
  transfers between devices with their start and end apart: 4, of which 2 were waited for; matrix products, arithmetic and copies ran while one was open for 0% of the time, Pallas kernels for 29%

profile of v2, /device:TPU:0, one launch (start us, length us, event | category | flops | bytes accessed | tf_op | source)
XLA Modules:
  0.0 68.5 jit_solution(14079379536959993533)
XLA Ops:
  0.6 1.3 %constant_dynamic-slice_fusion._ = bf16[1,32,32,512]{3,2,1,0:T(8,128)(2,1)S(1)} fusion(bf16[4,32,32,512]{3,2,1,0:T(8,128)(2,1)} %x_ref.3, s32[]{:T(128)S(6)} %select_n.3), kind=kLoop, calls=%fused_computation | loop fusion | bytes 2097156 | tf_op jit(solution)/shard_map/dynamic_slice | solution.py:547
  1.9 0.7 %collective-permute-start.1 = (bf16[1,32,32,512]{3,2,1,0:T(8,128)(2,1)S(1)}, bf16[1,32,32,512]{3,2,1,0:T(8,128)(2,1)S(1)}, u32[]{:S(2)}, u32[]{:S(2)}) collective-permute-start(bf16[1,32,32,512]{3,2,1,0:T(8,128)(2,1)S(1)} %constant_dynamic-slice_fusion._), channel_id=1, source_target_pairs={{1,2},{2,1},{3,4},{4,3},{5,6},{6,5},{7,8},{8,7},{9,10},{10,9},{11,... | collective-permute-start | bytes 3145736 | tf_op jit(solution)/shard_map/ppermute | solution.py:548
  2.7 0.0 copy-start
  2.7 2.2 %copy-done = bf16[4,32,32,512]{3,2,1,0:T(8,128)(2,1)S(1)} copy-done((bf16[4,32,32,512]{3,2,1,0:T(8,128)(2,1)S(1)}, bf16[4,32,32,512]{3,2,1,0:T(8,128)(2,1)}, u32[]{:S(2)}) %copy-start) | copy-done | bytes 4194328
  4.9 0.8 %copy-done.8 = f32[27,512]{1,0:T(8,128)S(1)} copy-done((f32[27,512]{1,0:T(8,128)S(1)}, f32[27,512]{1,0:T(8,128)}, u32[]{:S(2)}) %copy-start.8) | copy-done | bytes 55320
  5.7 4.0 %ends.1 = (bf16[1,32,32,512]{3,2,1,0:T(8,128)(2,1)S(1)}, bf16[2,1024,512]{2,1,0:T(8,128)(2,1)S(1)}) custom-call(s32[1]{0:T(128)} %bitcast.me_ref, bf16[1,32,32,512]{3,2,1,0:T(8,128)(2,1)S(1)} %constant_dynamic-slice_fusion._, bf16[4,32,32,512]{3,2,1,0:T(8,128)(2,1)S(1)} %copy-done, f32[27,512]{1,0:T(8,128)S(1)} %copy-done.8), custom_call_target="tpu_custom_call" | custom-call | flops 6291456000 | bytes 4194304 | tf_op jit(solution)/shard_map/ends/pallas_call | solution.py:149
  9.7 4.3 %collective-permute-start = (bf16[1,32,32,512]{3,2,1,0:T(8,128)(2,1)S(1)}, bf16[1,32,32,512]{3,2,1,0:T(8,128)(2,1)S(1)}, u32[]{:S(2)}, u32[]{:S(2)}) collective-permute-start(bf16[1,32,32,512]{3,2,1,0:T(8,128)(2,1)S(1)} %get-tuple-element.21), channel_id=1, source_target_pairs={{0,1},{1,0},{2,3},{3,2},{4,5},{5,4},{6,7},{7,6},{8,9},{9,8},{10,11... | collective-permute-start | bytes 3145736 | tf_op jit(solution)/shard_map/ppermute | solution.py:555
  14.0 10.8 %inside.1 = (bf16[2,1024,512]{2,1,0:T(8,128)(2,1)S(1)}, f32[512,512]{1,0:T(8,128)S(1)}, f32[512,128]{1,0:T(8,128)S(1)}, bf16[528,512]{1,0:T(8,128)(2,1)S(1)}) custom-call(bf16[4,32,32,512]{3,2,1,0:T(8,128)(2,1)S(1)} %copy-done, f32[27,512]{1,0:T(8,128)S(1)} %copy-done.9, bf16[512,512]{1,0:T(8,128)(2,1)S(1)} %copy-done.7, f32[1,512]{1,0:T(1,128)S(1)} %bitcast.12), custom_call_target="tpu_custom_call" | custom-call | flops 14680064000 | bytes 4194304 | tf_op jit(solution)/shard_map/inside/pallas_call | solution.py:236
  24.8 3.1 %near.1 = (bf16[1,1024,512]{2,1,0:T(8,128)(2,1)S(1)}, f32[512,512]{1,0:T(8,128)S(1)}, f32[512,128]{1,0:T(8,128)S(1)}) custom-call(s32[1]{0:T(128)} %bitcast.me_ref, bf16[1,32,32,512]{3,2,1,0:T(8,128)(2,1)S(1)} %collective-permute-done.halo_ref, bf16[2,1024,512]{2,1,0:T(8,128)(2,1)S(1)} %get-tuple-element.22.partial_ref, f32[27,512]{1,0:T(8,128)S(1)} %copy-done.9, ...), custom_call_target="tpu_custom_call" | custom-call | flops 8388608000 | bytes 2097152 | tf_op jit(solution)/shard_map/near/pallas_call | solution.py:366
  27.9 3.6 %far.1 = (bf16[512,1024]{1,0:T(8,128)(2,1)S(1)}, bf16[8,136,128]{2,1,0:T(8,128)(2,1)S(1)}, f32[512,512]{1,0:T(8,128)S(1)}, f32[512,128]{1,0:T(8,128)S(1)}, bf16[1024,512]{1,0:T(8,128)(2,1)S(1)}) custom-call(s32[1]{0:T(128)} %bitcast.me_ref, bf16[1,32,32,512]{3,2,1,0:T(8,128)(2,1)S(1)} %collective-permute-done.1.halo_ref, ...), custom_call_target="tpu_custom_call" | custom-call | flops 8388608000 | bytes 2097152 | tf_op jit(solution)/shard_map/far/pallas_call | solution.py:366
  31.5 0.0 copy-start.2
  31.5 0.0 copy-start.3
  31.6 0.0 copy-start.4
  31.6 0.0 copy-start.5
  31.6 2.0 %collective-permute-start.2 = (bf16[8,136,128]{2,1,0:T(8,128)(2,1)S(1)}, bf16[8,136,128]{2,1,0:T(8,128)(2,1)S(1)}, u32[]{:S(2)}, u32[]{:S(2)}) collective-permute-start(bf16[8,136,128]{2,1,0:T(8,128)(2,1)S(1)} %get-tuple-element.34), channel_id=1, source_target_pairs={{0,1},{1,0},{2,3},{3,2},{4,5},{5,4},{6,7},{7,6},{8,9},{9,8},{10,11... | collective-permute-start | bytes 835592 | tf_op jit(solution)/shard_map/ppermute | solution.py:566
  33.6 0.5 keep.1
  34.1 0.7 collective-permute-done.2.other_ref
  34.7 0.1 merge.1
  34.8 16.2 %all_to_all.10.parts_ref = bf16[8,136,128]{2,1,0:T(8,128)(2,1)S(1)} all-to-all(bf16[8,136,128]{2,1,0:T(8,128)(2,1)S(1)} %merge.1), channel_id=1, replica_groups={{0,2,4,6,8,10,12,14},{1,3,5,7,9,11,13,15},{16,18,20,22,24,26,28,30},{17..., dimensions={0} | all-to-all | bytes 557056 | tf_op jit(solution)/shard_map/all_to_all | solution.py:569
  51.1 1.6 %owner.1 = (bf16[32,512]{1,0:T(8,128)(2,1)}, bf16[8,32,512]{2,1,0:T(8,128)(2,1)S(1)}) custom-call(bf16[8,136,128]{2,1,0:T(8,128)(2,1)S(1)} %all_to_all.10.parts_ref, f32[1,512]{1,0:T(1,128)S(1)} %bitcast.11, bf16[512,512]{1,0:T(8,128)(2,1)S(1)} %copy-done.4, bf16[512,1024]{1,0:T(8,128)(2,1)S(1)} %copy-done.2, bf16[1024,512]{1,0:T(8,128)(2,1)S(1)} %copy-done.3, ...), custom_call_target="tpu_custom_call" | custom-call | tf_op jit(solution)/shard_map/owner/pallas_call | solution.py:429
  52.7 11.4 %all_to_all.11 = bf16[8,32,512]{2,1,0:T(8,128)(2,1)S(1)} all-to-all(bf16[8,32,512]{2,1,0:T(8,128)(2,1)S(1)} %get-tuple-element.35), channel_id=1, replica_groups={{0,2,4,6,8,10,12,14},{1,3,5,7,9,11,13,15},{16,18,20,22,24,26,28,30},{17..., dimensions={0} | all-to-all | bytes 524288 | tf_op jit(solution)/shard_map/all_to_all | solution.py:581
  64.0 1.3 %ahead.1.ahead_ref = f32[3,1024,512]{2,1,0:T(8,128)S(1)} custom-call(s32[1]{0:T(128)} %bitcast.me_ref, bf16[4,1024,512]{2,1,0:T(8,128)(2,1)S(1)} %bitcast.6, bf16[2,1024,512]{2,1,0:T(8,128)(2,1)S(1)} %get-tuple-element.20.inside_ref, bf16[1,1024,512]{2,1,0:T(8,128)(2,1)S(1)} %get-tuple-element.26.near_ref, bf16[256,512]{1,0:T(8,128)(2,1)S(1)} %bitcast.9), custom_call_target="tpu_custom_call" | custom-call | flops 1073741824 | bytes 8388608 | tf_op jit(solution)/shard_map/ahead/pallas_call | solution.py:460
  65.3 0.2 collective-permute-done.3.other_ref
  65.6 2.7 %update.1 = bf16[4,1024,512]{2,1,0:T(8,128)(2,1)} custom-call(s32[1]{0:T(128)} %bitcast.me_ref, bf16[4,1024,512]{2,1,0:T(8,128)(2,1)S(1)} %bitcast.7, f32[3,1024,512]{2,1,0:T(8,128)S(1)} %ahead.1.ahead_ref, bf16[2,1024,512]{2,1,0:T(8,128)(2,1)S(1)} %get-tuple-element.20.inside_ref, bf16[1,1024,512]{2,1,0:T(8,128)(2,1)S(1)} %get-tuple-element.26.near_ref, ...), custom_call_target="tpu_custom_call" | custom-call | tf_op jit(solution)/shard_map/update/pallas_call | solution.py:514
  (18 shorter events, 0.0 us)
Async XLA Ops:
  1.9 26.0 %collective-permute-start.1 = (bf16[1,32,32,512]{3,2,1,0:T(8,128)(2,1)S(1)}, bf16[1,32,32,512]{3,2,1,0:T(8,128)(2,1)S(1)}, u32[]{:S(2)}, u32[]{:S(2)}) collective-permute-start(bf16[1,32,32,512]{3,2,1,0:T(8,128)(2,1)S(1)} %constant_dynamic-slice_fusion._), channel_id=1, source_target_pairs={{1,2},{2,1},{3,4},{4,3},{5,6},{6,5},{7,8},{8,7},{9,10},{10,9},{11,... | collective-permute-start | bytes 3145736 | tf_op jit(solution)/shard_map/ppermute | solution.py:548
  2.7 2.2 %copy-start = (bf16[4,32,32,512]{3,2,1,0:T(8,128)(2,1)S(1)}, bf16[4,32,32,512]{3,2,1,0:T(8,128)(2,1)}, u32[]{:S(2)}) copy-start(bf16[4,32,32,512]{3,2,1,0:T(8,128)(2,1)} %x_ref.3) | copy-start | bytes 12582916
  4.9 0.8 %copy-start.8 = (f32[27,512]{1,0:T(8,128)S(1)}, f32[27,512]{1,0:T(8,128)}, u32[]{:S(2)}) copy-start(f32[27,512]{1,0:T(8,128)} %k_ref.7) | copy-start | bytes 165892
  5.7 8.3 %copy-start.7 = (bf16[512,512]{1,0:T(8,128)(2,1)S(1)}, bf16[512,512]{1,0:T(8,128)(2,1)}, u32[]{:S(2)}) copy-start(bf16[512,512]{1,0:T(8,128)(2,1)} %affinity_ref.1) | copy-start | bytes 1572868
  5.7 8.3 %copy-start.9 = (f32[27,512]{1,0:T(8,128)S(1)}, f32[27,512]{1,0:T(8,128)}, u32[]{:S(2)}) copy-start(f32[27,512]{1,0:T(8,128)} %k_ref.7) | copy-start | bytes 165892
  5.7 8.3 %copy-start.10 = (f32[512]{0:T(512)S(1)}, f32[512]{0:T(512)}, u32[]{:S(2)}) copy-start(f32[512]{0:T(512)} %param.12) | copy-start | bytes 6148
  9.7 15.1 %collective-permute-start = (bf16[1,32,32,512]{3,2,1,0:T(8,128)(2,1)S(1)}, bf16[1,32,32,512]{3,2,1,0:T(8,128)(2,1)S(1)}, u32[]{:S(2)}, u32[]{:S(2)}) collective-permute-start(bf16[1,32,32,512]{3,2,1,0:T(8,128)(2,1)S(1)} %get-tuple-element.21), channel_id=1, source_target_pairs={{0,1},{1,0},{2,3},{3,2},{4,5},{5,4},{6,7},{7,6},{8,9},{9,8},{10,11... | collective-permute-start | bytes 3145736 | tf_op jit(solution)/shard_map/ppermute | solution.py:555
  31.5 19.5 %copy-start.2 = (bf16[512,1024]{1,0:T(8,128)(2,1)S(1)}, bf16[512,1024]{1,0:T(8,128)(2,1)}, u32[]{:S(2)}) copy-start(bf16[512,1024]{1,0:T(8,128)(2,1)} %widening_ref.1) | copy-start | bytes 3145732
  31.5 19.5 %copy-start.3 = (bf16[1024,512]{1,0:T(8,128)(2,1)S(1)}, bf16[1024,512]{1,0:T(8,128)(2,1)}, u32[]{:S(2)}) copy-start(bf16[1024,512]{1,0:T(8,128)(2,1)} %narrowing_ref.1) | copy-start | bytes 3145732
  31.6 19.5 %copy-start.4 = (bf16[512,512]{1,0:T(8,128)(2,1)S(1)}, bf16[512,512]{1,0:T(8,128)(2,1)}, u32[]{:S(2)}) copy-start(bf16[512,512]{1,0:T(8,128)(2,1)} %content_ref.1) | copy-start | bytes 1572868
  31.6 19.5 %copy-start.5 = (bf16[512,512]{1,0:T(8,128)(2,1)S(1)}, bf16[512,512]{1,0:T(8,128)(2,1)}, u32[]{:S(2)}) copy-start(bf16[512,512]{1,0:T(8,128)(2,1)} %final_ref.1) | copy-start | bytes 1572868
  31.6 19.5 %copy-start.6 = (f32[512]{0:T(512)S(1)}, f32[512]{0:T(512)}, u32[]{:S(2)}) copy-start(f32[512]{0:T(512)} %param.14) | copy-start | bytes 6148
  31.6 3.2 %collective-permute-start.2 = (bf16[8,136,128]{2,1,0:T(8,128)(2,1)S(1)}, bf16[8,136,128]{2,1,0:T(8,128)(2,1)S(1)}, u32[]{:S(2)}, u32[]{:S(2)}) collective-permute-start(bf16[8,136,128]{2,1,0:T(8,128)(2,1)S(1)} %get-tuple-element.34), channel_id=1, source_target_pairs={{0,1},{1,0},{2,3},{3,2},{4,5},{5,4},{6,7},{7,6},{8,9},{9,8},{10,11... | collective-permute-start | bytes 835592 | tf_op jit(solution)/shard_map/ppermute | solution.py:566
  33.6 30.5 %copy-start.1 = (bf16[4,32,32,512]{3,2,1,0:T(8,128)(2,1)S(1)}, bf16[4,32,32,512]{3,2,1,0:T(8,128)(2,1)}, u32[]{:S(2)}) copy-start(bf16[4,32,32,512]{3,2,1,0:T(8,128)(2,1)} %x_ref.3) | copy-start | bytes 12582916
  64.0 1.5 %collective-permute-start.3 = (bf16[256,512]{1,0:T(8,128)(2,1)S(1)}, bf16[256,512]{1,0:T(8,128)(2,1)S(1)}, u32[]{:S(2)}, u32[]{:S(2)}) collective-permute-start(bf16[256,512]{1,0:T(8,128)(2,1)S(1)} %bitcast.8), channel_id=1, source_target_pairs={{0,1},{1,0},{2,3},{3,2},{4,5},{5,4},{6,7},{7,6},{8,9},{9,8},{10,11... | collective-permute-start | bytes 786440 | tf_op jit(solution)/shard_map/ppermute | solution.py:582

commit v3 on v2

--- a/solution.py
+++ b/solution.py
@@ -260,12 +260,12 @@
 
 def edge_kernel(is_far, me_ref, halo_ref, partial_ref, k_ref, map_ref, sums_in_ref, mass_in_ref, *rest):
     if is_far:
-        by_slice_ref, send_ref, sums_ref, mass_ref, hid_ref, taps_ref = rest
+        by_slice_ref, send_ref, mass_ref, hid_ref, taps_ref, sums_ref = rest
     else:
         probs_ref, sums_ref, mass_ref, taps_ref, hid_ref, by_slice_ref = rest
     _, height, depth, channels = halo_ref.shape
-    slices = sums_in_ref.shape[0]
     odd = me_ref[0] & 1
+    rows_of = half_of(1 - odd, sums_in_ref) if is_far else slice(None)
     side = odd if is_far else 1 - odd
     spread_taps(k_ref, [2 * side], taps_ref)
     mass_ref[...] = mass_in_ref[...]
@@ -298,28 +298,28 @@
             probs_ref[0, group] = by_slice.T
         by_slice_ref[:, group] = by_slice
         if group.stop == most:
-            sums_ref[...] = sums_in_ref[...] + dot(by_slice_ref[:, :most], hid_ref[:most])
-    if not is_far:
-        sums_ref[...] += dot(by_slice_ref[:, most:], hid_ref[most:])
-        return
-    write_share(1 - odd, cells, by_slice_ref, hid_ref, sums_ref, mass_ref, send_ref)
-
-
-def write_share(side, left, by_slice_ref, hid_ref, sums_ref, mass_ref, share_ref):
-    slices, channels = sums_ref.shape
-    most = hid_ref.shape[0] - left
+            sums_ref[...] = sums_in_ref[rows_of, :] + dot(by_slice_ref[rows_of, :most], hid_ref[:most])
+    total = sums_ref[...] + dot(by_slice_ref[rows_of, most:], hid_ref[most:])
+    if is_far:
+        write_share(total, mass_ref[rows_of, :], send_ref)
+    else:
+        sums_ref[...] = total
+
+
+def half_of(side, ref):
+    half = ref.shape[0] // 2
+    return pl.ds(pl.multiple_of(side * half, half), half)
+
+
+def write_share(total, mass, share_ref):
     owners, rows, _ = share_ref.shape
-    held = channels // LANES
+    held = total.shape[1] // LANES
     rows = (rows - 8) // held
-    start = pl.multiple_of(side * (slices // 2), slices // 2)
-    mine = pl.ds(start, slices // 2)
-    total = sums_ref[mine, :] + dot(by_slice_ref[mine, most:], hid_ref[most:])
     for i in range(held):
         part = total[:, i * LANES : (i + 1) * LANES].astype(share_ref.dtype)
         share_ref[:, i * rows : (i + 1) * rows, :] = part.reshape(owners, rows, LANES)
     tiles = rows // 8
     lane = lax.broadcasted_iota(jnp.int32, (8, LANES), 1)
-    mass = mass_ref[mine, :]
     for owner in range(owners):
         tail = None
         for g in range(tiles):
@@ -332,15 +332,17 @@
         share_ref[owner, held * rows :, :] = tail.astype(share_ref.dtype)
 
 
-def keep_kernel(left, me_ref, by_slice_ref, hid_ref, sums_ref, mass_ref, keep_ref, probs_ref):
-    write_share(me_ref[0] & 1, left, by_slice_ref, hid_ref, sums_ref, mass_ref, keep_ref)
+def keep_kernel(me_ref, by_slice_ref, hid_ref, sums_ref, mass_ref, keep_ref, probs_ref):
+    mine = half_of(me_ref[0] & 1, sums_ref)
+    total = sums_ref[mine, :] + dot(by_slice_ref[mine, :], hid_ref[...])
+    write_share(total, mass_ref[mine, :], keep_ref)
     probs_ref[0] = by_slice_ref[...].T
 
 
-def keep_call(me, by_slice, hid, sums, mass, shape, left):
+def keep_call(me, by_slice, hid, sums, mass, shape):
     slices, cells = by_slice.shape
     return pl.pallas_call(
-        functools.partial(keep_kernel, left),
+        keep_kernel,
         in_specs=[SMEM] + [VMEM] * 4,
         out_specs=[VMEM, VMEM],
         out_shape=[jax.ShapeDtypeStruct(shape, F32), jax.ShapeDtypeStruct((1, cells, slices), BF16)],
@@ -359,7 +361,8 @@
     scratch = [((9, REPEAT, channels), CONV)]
     if is_far:
         rows = channels // LANES * (slices // owners) + 8
-        outs = [by_slice, ((owners // 2, rows, LANES), BF16)] + carry + [hidden]
+        outs = [by_slice, ((owners // 2, rows, LANES), BF16), carry[1], hidden]
+        scratch += [((slices // 2, channels), F32)]
     else:
         outs = [((1, cells, slices), BF16)] + carry
         scratch += [hidden, by_slice]
@@ -559,12 +562,12 @@
     near_probs, sums, mass = edge_call(
         False, me, near_halo, taps, maps, partial, sums, mass, 2 * owners
     )
-    by_slice, send, sums, mass, hid = edge_call(
+    by_slice, send, mass, hid = edge_call(
         True, me, far_halo, taps, maps, partial, sums, mass, 2 * owners
     )
 
     received = lax.ppermute(send, "gx", near_pairs)
-    keep, far_probs = keep_call(me, by_slice, hid, sums, mass, send.shape, GROUP * depth)
+    keep, far_probs = keep_call(me, by_slice, hid, sums, mass, send.shape)
     parts = merge_call(keep, received)
     parts = lax.all_to_all(parts, "gx", 0, 0, axis_index_groups=groups)
     if share > 1:

time: 68.8 us -> 68.4 us (level)
  no operation moved by 1% of the time
where the time goes in v3:
time: 68.4 us; the launch traced here: 68.1 us
  blocking collectives  27.7 us (40%)
  Pallas kernels  27.3 us (40%)
  starting transfers between devices  6.97 us (10%)
  local copies, waits for them, and re-layouts  4.37 us (6%)
  waiting for transfers between devices  0.89 us (1%)
  between operations  0.78 us (1%)
    all_to_all x1, blocking collectives, per_device(): parts = lax.all_to_all(parts, 'gx', 0, 0, axis_index_groups=groups)  16.3 us
    all_to_all x1, blocking collectives, per_device(): lax.all_to_all(mapped, 'gx', 0, 0, axis_index_groups=groups)  11.4 us
    pallas_call x1, Pallas kernels, inside_call(): pl.pallas_call(functools.partial(inside_kernel, bits), in_specs=[VMEM] *...  10.8 us
    pallas_call x2, Pallas kernels, edge_call(): pl.pallas_call(functools.partial(edge_kernel, is_far), in_specs=[SMEM] +...  6.37 us
    ppermute x1, starting transfers between devices, per_device(): near_halo = lax.ppermute(near_plane, 'gx', near_pairs)  4.3 us
    pallas_call x1, Pallas kernels, ends_call(): pl.pallas_call(ends_kernel, in_specs=[SMEM, pl.BlockSpec(memory_space=pl....  3.99 us
    unnamed x22, local copies, waits for them, and re-layouts  3.07 us
    pallas_call x1, Pallas kernels, update_call(): pl.pallas_call(update_kernel, in_specs=[SMEM] + [VMEM] * 7, out_specs=HBM...  2.73 us
  transfers between devices with their start and end apart: 4, of which 2 were waited for; matrix products, arithmetic and copies ran while one was open for 0% of the time, Pallas kernels for 29%

profile of v3, /device:TPU:0, one launch (start us, length us, event | category | flops | bytes accessed | tf_op | source)
XLA Modules:
  0.0 68.1 jit_solution(15895191713186969685)
XLA Ops:
  0.6 1.3 %constant_dynamic-slice_fusion._ = bf16[1,32,32,512]{3,2,1,0:T(8,128)(2,1)S(1)} fusion(bf16[4,32,32,512]{3,2,1,0:T(8,128)(2,1)} %x_ref.3, s32[]{:T(128)S(6)} %select_n.3), kind=kLoop, calls=%fused_computation | loop fusion | bytes 2097156 | tf_op jit(solution)/shard_map/dynamic_slice | solution.py:550
  1.9 0.7 %collective-permute-start.1 = (bf16[1,32,32,512]{3,2,1,0:T(8,128)(2,1)S(1)}, bf16[1,32,32,512]{3,2,1,0:T(8,128)(2,1)S(1)}, u32[]{:S(2)}, u32[]{:S(2)}) collective-permute-start(bf16[1,32,32,512]{3,2,1,0:T(8,128)(2,1)S(1)} %constant_dynamic-slice_fusion._), channel_id=1, source_target_pairs={{1,2},{2,1},{3,4},{4,3},{5,6},{6,5},{7,8},{8,7},{9,10},{10,9},{11,... | collective-permute-start | bytes 3145736 | tf_op jit(solution)/shard_map/ppermute | solution.py:551
  2.7 0.0 copy-start
  2.7 2.2 %copy-done = bf16[4,32,32,512]{3,2,1,0:T(8,128)(2,1)S(1)} copy-done((bf16[4,32,32,512]{3,2,1,0:T(8,128)(2,1)S(1)}, bf16[4,32,32,512]{3,2,1,0:T(8,128)(2,1)}, u32[]{:S(2)}) %copy-start) | copy-done | bytes 4194328
  4.9 0.8 %copy-done.8 = f32[27,512]{1,0:T(8,128)S(1)} copy-done((f32[27,512]{1,0:T(8,128)S(1)}, f32[27,512]{1,0:T(8,128)}, u32[]{:S(2)}) %copy-start.8) | copy-done | bytes 55320
  5.7 4.0 %ends.1 = (bf16[1,32,32,512]{3,2,1,0:T(8,128)(2,1)S(1)}, bf16[2,1024,512]{2,1,0:T(8,128)(2,1)S(1)}) custom-call(s32[1]{0:T(128)} %bitcast.me_ref, bf16[1,32,32,512]{3,2,1,0:T(8,128)(2,1)S(1)} %constant_dynamic-slice_fusion._, bf16[4,32,32,512]{3,2,1,0:T(8,128)(2,1)S(1)} %copy-done, f32[27,512]{1,0:T(8,128)S(1)} %copy-done.8), custom_call_target="tpu_custom_call" | custom-call | flops 6291456000 | bytes 4194304 | tf_op jit(solution)/shard_map/ends/pallas_call | solution.py:149
  9.7 4.3 %collective-permute-start = (bf16[1,32,32,512]{3,2,1,0:T(8,128)(2,1)S(1)}, bf16[1,32,32,512]{3,2,1,0:T(8,128)(2,1)S(1)}, u32[]{:S(2)}, u32[]{:S(2)}) collective-permute-start(bf16[1,32,32,512]{3,2,1,0:T(8,128)(2,1)S(1)} %get-tuple-element.20), channel_id=1, source_target_pairs={{0,1},{1,0},{2,3},{3,2},{4,5},{5,4},{6,7},{7,6},{8,9},{9,8},{10,11... | collective-permute-start | bytes 3145736 | tf_op jit(solution)/shard_map/ppermute | solution.py:558
  14.0 10.8 %inside.1 = (bf16[2,1024,512]{2,1,0:T(8,128)(2,1)S(1)}, f32[512,512]{1,0:T(8,128)S(1)}, f32[512,128]{1,0:T(8,128)S(1)}, bf16[528,512]{1,0:T(8,128)(2,1)S(1)}) custom-call(bf16[4,32,32,512]{3,2,1,0:T(8,128)(2,1)S(1)} %copy-done, f32[27,512]{1,0:T(8,128)S(1)} %copy-done.9, bf16[512,512]{1,0:T(8,128)(2,1)S(1)} %copy-done.7, f32[1,512]{1,0:T(1,128)S(1)} %bitcast.12), custom_call_target="tpu_custom_call" | custom-call | flops 14680064000 | bytes 4194304 | tf_op jit(solution)/shard_map/inside/pallas_call | solution.py:236
  24.8 3.1 %near.1 = (bf16[1,1024,512]{2,1,0:T(8,128)(2,1)S(1)}, f32[512,512]{1,0:T(8,128)S(1)}, f32[512,128]{1,0:T(8,128)S(1)}) custom-call(s32[1]{0:T(128)} %bitcast.me_ref, bf16[1,32,32,512]{3,2,1,0:T(8,128)(2,1)S(1)} %collective-permute-done.halo_ref, bf16[2,1024,512]{2,1,0:T(8,128)(2,1)S(1)} %get-tuple-element.21.partial_ref, f32[27,512]{1,0:T(8,128)S(1)} %copy-done.9, ...), custom_call_target="tpu_custom_call" | custom-call | flops 8388608000 | bytes 2097152 | tf_op jit(solution)/shard_map/near/pallas_call | solution.py:369
  28.0 3.2 %far.1 = (bf16[512,1024]{1,0:T(8,128)(2,1)S(1)}, bf16[8,136,128]{2,1,0:T(8,128)(2,1)S(1)}, f32[512,128]{1,0:T(8,128)S(1)}, bf16[1024,512]{1,0:T(8,128)(2,1)S(1)}) custom-call(s32[1]{0:T(128)} %bitcast.me_ref, bf16[1,32,32,512]{3,2,1,0:T(8,128)(2,1)S(1)} %collective-permute-done.1.halo_ref, bf16[2,1024,512]{2,1,0:T(8,128)(2,1)S(1)} %get-tuple-element.21.partial_ref, ...), custom_call_target="tpu_custom_call" | custom-call | flops 8388608000 | bytes 2097152 | tf_op jit(solution)/shard_map/far/pallas_call | solution.py:369
  31.2 0.0 copy-start.2
  31.2 0.0 copy-start.3
  31.2 0.0 copy-start.4
  31.3 0.0 copy-start.5
  31.3 0.0 copy-start.6
  31.3 1.9 %collective-permute-start.2 = (bf16[8,136,128]{2,1,0:T(8,128)(2,1)S(1)}, bf16[8,136,128]{2,1,0:T(8,128)(2,1)S(1)}, u32[]{:S(2)}, u32[]{:S(2)}) collective-permute-start(bf16[8,136,128]{2,1,0:T(8,128)(2,1)S(1)} %get-tuple-element.32), channel_id=1, source_target_pairs={{0,1},{1,0},{2,3},{3,2},{4,5},{5,4},{6,7},{7,6},{8,9},{9,8},{10,11... | collective-permute-start | bytes 835592 | tf_op jit(solution)/shard_map/ppermute | solution.py:569
  33.2 0.5 keep.1
  33.8 0.6 collective-permute-done.2.other_ref
  34.5 16.3 %all_to_all.10.parts_ref = bf16[8,136,128]{2,1,0:T(8,128)(2,1)S(1)} all-to-all(bf16[8,136,128]{2,1,0:T(8,128)(2,1)S(1)} %merge.1), channel_id=1, replica_groups={{0,2,4,6,8,10,12,14},{1,3,5,7,9,11,13,15},{16,18,20,22,24,26,28,30},{17..., dimensions={0} | all-to-all | bytes 557056 | tf_op jit(solution)/shard_map/all_to_all | solution.py:572
  50.8 1.6 %owner.1 = (bf16[32,512]{1,0:T(8,128)(2,1)}, bf16[8,32,512]{2,1,0:T(8,128)(2,1)S(1)}) custom-call(bf16[8,136,128]{2,1,0:T(8,128)(2,1)S(1)} %all_to_all.10.parts_ref, f32[1,512]{1,0:T(1,128)S(1)} %bitcast.11, bf16[512,512]{1,0:T(8,128)(2,1)S(1)} %copy-done.4, bf16[512,1024]{1,0:T(8,128)(2,1)S(1)} %copy-done.2, bf16[1024,512]{1,0:T(8,128)(2,1)S(1)} %copy-done.3, ...), custom_call_target="tpu_custom_call" | custom-call | tf_op jit(solution)/shard_map/owner/pallas_call | solution.py:432
  52.4 11.4 %all_to_all.11 = bf16[8,32,512]{2,1,0:T(8,128)(2,1)S(1)} all-to-all(bf16[8,32,512]{2,1,0:T(8,128)(2,1)S(1)} %get-tuple-element.33), channel_id=1, replica_groups={{0,2,4,6,8,10,12,14},{1,3,5,7,9,11,13,15},{16,18,20,22,24,26,28,30},{17..., dimensions={0} | all-to-all | bytes 524288 | tf_op jit(solution)/shard_map/all_to_all | solution.py:584
  63.8 1.3 %ahead.1.ahead_ref = f32[3,1024,512]{2,1,0:T(8,128)S(1)} custom-call(s32[1]{0:T(128)} %bitcast.me_ref, bf16[4,1024,512]{2,1,0:T(8,128)(2,1)S(1)} %bitcast.6, bf16[2,1024,512]{2,1,0:T(8,128)(2,1)S(1)} %get-tuple-element.19.inside_ref, bf16[1,1024,512]{2,1,0:T(8,128)(2,1)S(1)} %get-tuple-element.25.near_ref, bf16[256,512]{1,0:T(8,128)(2,1)S(1)} %bitcast.9), custom_call_target="tpu_custom_call" | custom-call | flops 1073741824 | bytes 8388608 | tf_op jit(solution)/shard_map/ahead/pallas_call | solution.py:463
  65.1 0.2 collective-permute-done.3.other_ref
  65.4 2.7 %update.1 = bf16[4,1024,512]{2,1,0:T(8,128)(2,1)} custom-call(s32[1]{0:T(128)} %bitcast.me_ref, bf16[4,1024,512]{2,1,0:T(8,128)(2,1)S(1)} %bitcast.7, f32[3,1024,512]{2,1,0:T(8,128)S(1)} %ahead.1.ahead_ref, bf16[2,1024,512]{2,1,0:T(8,128)(2,1)S(1)} %get-tuple-element.19.inside_ref, bf16[1,1024,512]{2,1,0:T(8,128)(2,1)S(1)} %get-tuple-element.25.near_ref, ...), custom_call_target="tpu_custom_call" | custom-call | tf_op jit(solution)/shard_map/update/pallas_call | solution.py:517
  (18 shorter events, 0.1 us)
Async XLA Ops:
  1.9 26.0 %collective-permute-start.1 = (bf16[1,32,32,512]{3,2,1,0:T(8,128)(2,1)S(1)}, bf16[1,32,32,512]{3,2,1,0:T(8,128)(2,1)S(1)}, u32[]{:S(2)}, u32[]{:S(2)}) collective-permute-start(bf16[1,32,32,512]{3,2,1,0:T(8,128)(2,1)S(1)} %constant_dynamic-slice_fusion._), channel_id=1, source_target_pairs={{1,2},{2,1},{3,4},{4,3},{5,6},{6,5},{7,8},{8,7},{9,10},{10,9},{11,... | collective-permute-start | bytes 3145736 | tf_op jit(solution)/shard_map/ppermute | solution.py:551
  2.7 2.2 %copy-start = (bf16[4,32,32,512]{3,2,1,0:T(8,128)(2,1)S(1)}, bf16[4,32,32,512]{3,2,1,0:T(8,128)(2,1)}, u32[]{:S(2)}) copy-start(bf16[4,32,32,512]{3,2,1,0:T(8,128)(2,1)} %x_ref.3) | copy-start | bytes 12582916
  4.9 0.8 %copy-start.8 = (f32[27,512]{1,0:T(8,128)S(1)}, f32[27,512]{1,0:T(8,128)}, u32[]{:S(2)}) copy-start(f32[27,512]{1,0:T(8,128)} %k_ref.7) | copy-start | bytes 165892
  5.7 8.3 %copy-start.7 = (bf16[512,512]{1,0:T(8,128)(2,1)S(1)}, bf16[512,512]{1,0:T(8,128)(2,1)}, u32[]{:S(2)}) copy-start(bf16[512,512]{1,0:T(8,128)(2,1)} %affinity_ref.1) | copy-start | bytes 1572868
  5.7 8.3 %copy-start.9 = (f32[27,512]{1,0:T(8,128)S(1)}, f32[27,512]{1,0:T(8,128)}, u32[]{:S(2)}) copy-start(f32[27,512]{1,0:T(8,128)} %k_ref.7) | copy-start | bytes 165892
  5.7 8.3 %copy-start.10 = (f32[512]{0:T(512)S(1)}, f32[512]{0:T(512)}, u32[]{:S(2)}) copy-start(f32[512]{0:T(512)} %param.12) | copy-start | bytes 6148
  9.7 15.1 %collective-permute-start = (bf16[1,32,32,512]{3,2,1,0:T(8,128)(2,1)S(1)}, bf16[1,32,32,512]{3,2,1,0:T(8,128)(2,1)S(1)}, u32[]{:S(2)}, u32[]{:S(2)}) collective-permute-start(bf16[1,32,32,512]{3,2,1,0:T(8,128)(2,1)S(1)} %get-tuple-element.20), channel_id=1, source_target_pairs={{0,1},{1,0},{2,3},{3,2},{4,5},{5,4},{6,7},{7,6},{8,9},{9,8},{10,11... | collective-permute-start | bytes 3145736 | tf_op jit(solution)/shard_map/ppermute | solution.py:558
  31.2 19.6 %copy-start.2 = (bf16[512,1024]{1,0:T(8,128)(2,1)S(1)}, bf16[512,1024]{1,0:T(8,128)(2,1)}, u32[]{:S(2)}) copy-start(bf16[512,1024]{1,0:T(8,128)(2,1)} %widening_ref.1) | copy-start | bytes 3145732
  31.2 19.6 %copy-start.3 = (bf16[1024,512]{1,0:T(8,128)(2,1)S(1)}, bf16[1024,512]{1,0:T(8,128)(2,1)}, u32[]{:S(2)}) copy-start(bf16[1024,512]{1,0:T(8,128)(2,1)} %narrowing_ref.1) | copy-start | bytes 3145732
  31.2 19.5 %copy-start.4 = (bf16[512,512]{1,0:T(8,128)(2,1)S(1)}, bf16[512,512]{1,0:T(8,128)(2,1)}, u32[]{:S(2)}) copy-start(bf16[512,512]{1,0:T(8,128)(2,1)} %content_ref.1) | copy-start | bytes 1572868
  31.3 19.5 %copy-start.5 = (bf16[512,512]{1,0:T(8,128)(2,1)S(1)}, bf16[512,512]{1,0:T(8,128)(2,1)}, u32[]{:S(2)}) copy-start(bf16[512,512]{1,0:T(8,128)(2,1)} %final_ref.1) | copy-start | bytes 1572868
  31.3 19.5 %copy-start.6 = (f32[512]{0:T(512)S(1)}, f32[512]{0:T(512)}, u32[]{:S(2)}) copy-start(f32[512]{0:T(512)} %param.14) | copy-start | bytes 6148
  31.3 3.1 %collective-permute-start.2 = (bf16[8,136,128]{2,1,0:T(8,128)(2,1)S(1)}, bf16[8,136,128]{2,1,0:T(8,128)(2,1)S(1)}, u32[]{:S(2)}, u32[]{:S(2)}) collective-permute-start(bf16[8,136,128]{2,1,0:T(8,128)(2,1)S(1)} %get-tuple-element.32), channel_id=1, source_target_pairs={{0,1},{1,0},{2,3},{3,2},{4,5},{5,4},{6,7},{7,6},{8,9},{9,8},{10,11... | collective-permute-start | bytes 835592 | tf_op jit(solution)/shard_map/ppermute | solution.py:569
  33.2 30.6 %copy-start.1 = (bf16[4,32,32,512]{3,2,1,0:T(8,128)(2,1)S(1)}, bf16[4,32,32,512]{3,2,1,0:T(8,128)(2,1)}, u32[]{:S(2)}) copy-start(bf16[4,32,32,512]{3,2,1,0:T(8,128)(2,1)} %x_ref.3) | copy-start | bytes 12582916
  63.8 1.5 %collective-permute-start.3 = (bf16[256,512]{1,0:T(8,128)(2,1)S(1)}, bf16[256,512]{1,0:T(8,128)(2,1)S(1)}, u32[]{:S(2)}, u32[]{:S(2)}) collective-permute-start(bf16[256,512]{1,0:T(8,128)(2,1)S(1)} %bitcast.8), channel_id=1, source_target_pairs={{0,1},{1,0},{2,3},{3,2},{4,5},{5,4},{6,7},{7,6},{8,9},{9,8},{10,11... | collective-permute-start | bytes 786440 | tf_op jit(solution)/shard_map/ppermute | solution.py:585

commit v4 on v3

--- a/solution.py
+++ b/solution.py
@@ -57,13 +57,14 @@
     position = lax.broadcasted_iota(jnp.int32, (8, width), 0)
     results = []
     for out in range(count):
-        before, here, after = (s.astype(F32).reshape(depth, width) for s in sums[out])
+        before, after = (sums[out][c].astype(F32).reshape(depth, width) for c in (0, 2))
+        here = sums[out][1].reshape(depth, width)
         before, after = pltpu.roll(before, 1, 0), pltpu.roll(after, depth - 1, 0)
         low = jnp.where(position == 0, 0.0, before[:8])
         high = jnp.where(position == 7, 0.0, after[depth - 8 :])
         before = jnp.concatenate([low, before[8:]], axis=0)
         after = jnp.concatenate([after[: depth - 8], high], axis=0)
-        results.append(here + before + after)
+        results.append(here + (before + after).astype(CONV))
     return results
 
 

time: 68.4 us -> 68.3 us (level)
  transfers between devices with their start and end apart: 4 -> 4, of which waited for: 2 -> 2; matrix products, arithmetic and copies ran while one was open for 0% -> 0% of each run, Pallas kernels for 29% -> 28%
where the time goes in v4:
time: 68.3 us; the launch traced here: 68 us
  blocking collectives  27.7 us (41%)
  Pallas kernels  26.7 us (39%)
  starting transfers between devices  7.51 us (11%)
  local copies, waits for them, and re-layouts  4.37 us (6%)
  waiting for transfers between devices  0.89 us (1%)
  between operations  0.78 us (1%)
    all_to_all x1, blocking collectives, per_device(): parts = lax.all_to_all(parts, 'gx', 0, 0, axis_index_groups=groups)  16.3 us
    all_to_all x1, blocking collectives, per_device(): lax.all_to_all(mapped, 'gx', 0, 0, axis_index_groups=groups)  11.4 us
    pallas_call x1, Pallas kernels, inside_call(): pl.pallas_call(functools.partial(inside_kernel, bits), in_specs=[VMEM] *...  10.6 us
    pallas_call x2, Pallas kernels, edge_call(): pl.pallas_call(functools.partial(edge_kernel, is_far), in_specs=[SMEM] +...  6.22 us
    ppermute x1, starting transfers between devices, per_device(): near_halo = lax.ppermute(near_plane, 'gx', near_pairs)  4.3 us
    pallas_call x1, Pallas kernels, ends_call(): pl.pallas_call(ends_kernel, in_specs=[SMEM, pl.BlockSpec(memory_space=pl....  3.7 us
    unnamed x22, local copies, waits for them, and re-layouts  3.07 us
    pallas_call x1, Pallas kernels, update_call(): pl.pallas_call(update_kernel, in_specs=[SMEM] + [VMEM] * 7, out_specs=HBM...  2.73 us
  transfers between devices with their start and end apart: 4, of which 2 were waited for; matrix products, arithmetic and copies ran while one was open for 0% of the time, Pallas kernels for 28%

profile of v4, /device:TPU:0, one launch (start us, length us, event | category | flops | bytes accessed | tf_op | source)
XLA Modules:
  0.0 68.0 jit_solution(893787916122730030)
XLA Ops:
  0.6 1.3 %constant_dynamic-slice_fusion._ = bf16[1,32,32,512]{3,2,1,0:T(8,128)(2,1)S(1)} fusion(bf16[4,32,32,512]{3,2,1,0:T(8,128)(2,1)} %x_ref.3, s32[]{:T(128)S(6)} %select_n.3), kind=kLoop, calls=%fused_computation | loop fusion | bytes 2097156 | tf_op jit(solution)/shard_map/dynamic_slice | solution.py:551
  1.9 0.7 %collective-permute-start.1 = (bf16[1,32,32,512]{3,2,1,0:T(8,128)(2,1)S(1)}, bf16[1,32,32,512]{3,2,1,0:T(8,128)(2,1)S(1)}, u32[]{:S(2)}, u32[]{:S(2)}) collective-permute-start(bf16[1,32,32,512]{3,2,1,0:T(8,128)(2,1)S(1)} %constant_dynamic-slice_fusion._), channel_id=1, source_target_pairs={{1,2},{2,1},{3,4},{4,3},{5,6},{6,5},{7,8},{8,7},{9,10},{10,9},{11,... | collective-permute-start | bytes 3145736 | tf_op jit(solution)/shard_map/ppermute | solution.py:552
  2.7 0.0 copy-start
  2.7 2.2 %copy-done = bf16[4,32,32,512]{3,2,1,0:T(8,128)(2,1)S(1)} copy-done((bf16[4,32,32,512]{3,2,1,0:T(8,128)(2,1)S(1)}, bf16[4,32,32,512]{3,2,1,0:T(8,128)(2,1)}, u32[]{:S(2)}) %copy-start) | copy-done | bytes 4194328
  4.9 0.8 %copy-done.8 = f32[27,512]{1,0:T(8,128)S(1)} copy-done((f32[27,512]{1,0:T(8,128)S(1)}, f32[27,512]{1,0:T(8,128)}, u32[]{:S(2)}) %copy-start.8) | copy-done | bytes 55320
  5.7 3.7 %ends.1 = (bf16[1,32,32,512]{3,2,1,0:T(8,128)(2,1)S(1)}, bf16[2,1024,512]{2,1,0:T(8,128)(2,1)S(1)}) custom-call(s32[1]{0:T(128)} %bitcast.me_ref, bf16[1,32,32,512]{3,2,1,0:T(8,128)(2,1)S(1)} %constant_dynamic-slice_fusion._, bf16[4,32,32,512]{3,2,1,0:T(8,128)(2,1)S(1)} %copy-done, f32[27,512]{1,0:T(8,128)S(1)} %copy-done.8), custom_call_target="tpu_custom_call" | custom-call | flops 6291456000 | bytes 4194304 | tf_op jit(solution)/shard_map/ends/pallas_call | solution.py:150
  9.4 4.3 %collective-permute-start = (bf16[1,32,32,512]{3,2,1,0:T(8,128)(2,1)S(1)}, bf16[1,32,32,512]{3,2,1,0:T(8,128)(2,1)S(1)}, u32[]{:S(2)}, u32[]{:S(2)}) collective-permute-start(bf16[1,32,32,512]{3,2,1,0:T(8,128)(2,1)S(1)} %get-tuple-element.20), channel_id=1, source_target_pairs={{0,1},{1,0},{2,3},{3,2},{4,5},{5,4},{6,7},{7,6},{8,9},{9,8},{10,11... | collective-permute-start | bytes 3145736 | tf_op jit(solution)/shard_map/ppermute | solution.py:559
  13.7 10.6 %inside.1 = (bf16[2,1024,512]{2,1,0:T(8,128)(2,1)S(1)}, f32[512,512]{1,0:T(8,128)S(1)}, f32[512,128]{1,0:T(8,128)S(1)}, bf16[528,512]{1,0:T(8,128)(2,1)S(1)}) custom-call(bf16[4,32,32,512]{3,2,1,0:T(8,128)(2,1)S(1)} %copy-done, f32[27,512]{1,0:T(8,128)S(1)} %copy-done.9, bf16[512,512]{1,0:T(8,128)(2,1)S(1)} %copy-done.7, f32[1,512]{1,0:T(1,128)S(1)} %bitcast.12), custom_call_target="tpu_custom_call" | custom-call | flops 14680064000 | bytes 4194304 | tf_op jit(solution)/shard_map/inside/pallas_call | solution.py:237
  24.4 3.1 %near.1 = (bf16[1,1024,512]{2,1,0:T(8,128)(2,1)S(1)}, f32[512,512]{1,0:T(8,128)S(1)}, f32[512,128]{1,0:T(8,128)S(1)}) custom-call(s32[1]{0:T(128)} %bitcast.me_ref, bf16[1,32,32,512]{3,2,1,0:T(8,128)(2,1)S(1)} %collective-permute-done.halo_ref, bf16[2,1024,512]{2,1,0:T(8,128)(2,1)S(1)} %get-tuple-element.21.partial_ref, f32[27,512]{1,0:T(8,128)S(1)} %copy-done.9, ...), custom_call_target="tpu_custom_call" | custom-call | flops 8388608000 | bytes 2097152 | tf_op jit(solution)/shard_map/near/pallas_call | solution.py:370
  27.4 3.2 %far.1 = (bf16[512,1024]{1,0:T(8,128)(2,1)S(1)}, bf16[8,136,128]{2,1,0:T(8,128)(2,1)S(1)}, f32[512,128]{1,0:T(8,128)S(1)}, bf16[1024,512]{1,0:T(8,128)(2,1)S(1)}) custom-call(s32[1]{0:T(128)} %bitcast.me_ref, bf16[1,32,32,512]{3,2,1,0:T(8,128)(2,1)S(1)} %collective-permute-done.1.halo_ref, bf16[2,1024,512]{2,1,0:T(8,128)(2,1)S(1)} %get-tuple-element.21.partial_ref, ...), custom_call_target="tpu_custom_call" | custom-call | flops 8388608000 | bytes 2097152 | tf_op jit(solution)/shard_map/far/pallas_call | solution.py:370
  30.6 0.0 copy-start.2
  30.6 0.0 copy-start.3
  30.6 0.0 copy-start.4
  30.6 0.0 copy-start.5
  30.7 0.0 copy-start.6
  30.7 2.5 %collective-permute-start.2 = (bf16[8,136,128]{2,1,0:T(8,128)(2,1)S(1)}, bf16[8,136,128]{2,1,0:T(8,128)(2,1)S(1)}, u32[]{:S(2)}, u32[]{:S(2)}) collective-permute-start(bf16[8,136,128]{2,1,0:T(8,128)(2,1)S(1)} %get-tuple-element.32), channel_id=1, source_target_pairs={{0,1},{1,0},{2,3},{3,2},{4,5},{5,4},{6,7},{7,6},{8,9},{9,8},{10,11... | collective-permute-start | bytes 835592 | tf_op jit(solution)/shard_map/ppermute | solution.py:570
  33.1 0.5 keep.1
  33.7 0.6 collective-permute-done.2.other_ref
  34.4 16.3 %all_to_all.10.parts_ref = bf16[8,136,128]{2,1,0:T(8,128)(2,1)S(1)} all-to-all(bf16[8,136,128]{2,1,0:T(8,128)(2,1)S(1)} %merge.1), channel_id=1, replica_groups={{0,2,4,6,8,10,12,14},{1,3,5,7,9,11,13,15},{16,18,20,22,24,26,28,30},{17..., dimensions={0} | all-to-all | bytes 557056 | tf_op jit(solution)/shard_map/all_to_all | solution.py:573
  50.7 1.6 %owner.1 = (bf16[32,512]{1,0:T(8,128)(2,1)}, bf16[8,32,512]{2,1,0:T(8,128)(2,1)S(1)}) custom-call(bf16[8,136,128]{2,1,0:T(8,128)(2,1)S(1)} %all_to_all.10.parts_ref, f32[1,512]{1,0:T(1,128)S(1)} %bitcast.11, bf16[512,512]{1,0:T(8,128)(2,1)S(1)} %copy-done.4, bf16[512,1024]{1,0:T(8,128)(2,1)S(1)} %copy-done.2, bf16[1024,512]{1,0:T(8,128)(2,1)S(1)} %copy-done.3, ...), custom_call_target="tpu_custom_call" | custom-call | tf_op jit(solution)/shard_map/owner/pallas_call | solution.py:433
  52.3 11.4 %all_to_all.11 = bf16[8,32,512]{2,1,0:T(8,128)(2,1)S(1)} all-to-all(bf16[8,32,512]{2,1,0:T(8,128)(2,1)S(1)} %get-tuple-element.33), channel_id=1, replica_groups={{0,2,4,6,8,10,12,14},{1,3,5,7,9,11,13,15},{16,18,20,22,24,26,28,30},{17..., dimensions={0} | all-to-all | bytes 524288 | tf_op jit(solution)/shard_map/all_to_all | solution.py:585
  63.8 1.3 %ahead.1.ahead_ref = f32[3,1024,512]{2,1,0:T(8,128)S(1)} custom-call(s32[1]{0:T(128)} %bitcast.me_ref, bf16[4,1024,512]{2,1,0:T(8,128)(2,1)S(1)} %bitcast.6, bf16[2,1024,512]{2,1,0:T(8,128)(2,1)S(1)} %get-tuple-element.19.inside_ref, bf16[1,1024,512]{2,1,0:T(8,128)(2,1)S(1)} %get-tuple-element.25.near_ref, bf16[256,512]{1,0:T(8,128)(2,1)S(1)} %bitcast.9), custom_call_target="tpu_custom_call" | custom-call | flops 1073741824 | bytes 8388608 | tf_op jit(solution)/shard_map/ahead/pallas_call | solution.py:464
  65.0 0.2 collective-permute-done.3.other_ref
  65.3 2.7 %update.1 = bf16[4,1024,512]{2,1,0:T(8,128)(2,1)} custom-call(s32[1]{0:T(128)} %bitcast.me_ref, bf16[4,1024,512]{2,1,0:T(8,128)(2,1)S(1)} %bitcast.7, f32[3,1024,512]{2,1,0:T(8,128)S(1)} %ahead.1.ahead_ref, bf16[2,1024,512]{2,1,0:T(8,128)(2,1)S(1)} %get-tuple-element.19.inside_ref, bf16[1,1024,512]{2,1,0:T(8,128)(2,1)S(1)} %get-tuple-element.25.near_ref, ...), custom_call_target="tpu_custom_call" | custom-call | tf_op jit(solution)/shard_map/update/pallas_call | solution.py:518
  (18 shorter events, 0.1 us)
Async XLA Ops:
  1.9 25.5 %collective-permute-start.1 = (bf16[1,32,32,512]{3,2,1,0:T(8,128)(2,1)S(1)}, bf16[1,32,32,512]{3,2,1,0:T(8,128)(2,1)S(1)}, u32[]{:S(2)}, u32[]{:S(2)}) collective-permute-start(bf16[1,32,32,512]{3,2,1,0:T(8,128)(2,1)S(1)} %constant_dynamic-slice_fusion._), channel_id=1, source_target_pairs={{1,2},{2,1},{3,4},{4,3},{5,6},{6,5},{7,8},{8,7},{9,10},{10,9},{11,... | collective-permute-start | bytes 3145736 | tf_op jit(solution)/shard_map/ppermute | solution.py:552
  2.7 2.2 %copy-start = (bf16[4,32,32,512]{3,2,1,0:T(8,128)(2,1)S(1)}, bf16[4,32,32,512]{3,2,1,0:T(8,128)(2,1)}, u32[]{:S(2)}) copy-start(bf16[4,32,32,512]{3,2,1,0:T(8,128)(2,1)} %x_ref.3) | copy-start | bytes 12582916
  4.9 0.8 %copy-start.8 = (f32[27,512]{1,0:T(8,128)S(1)}, f32[27,512]{1,0:T(8,128)}, u32[]{:S(2)}) copy-start(f32[27,512]{1,0:T(8,128)} %k_ref.7) | copy-start | bytes 165892
  5.7 8.0 %copy-start.7 = (bf16[512,512]{1,0:T(8,128)(2,1)S(1)}, bf16[512,512]{1,0:T(8,128)(2,1)}, u32[]{:S(2)}) copy-start(bf16[512,512]{1,0:T(8,128)(2,1)} %affinity_ref.1) | copy-start | bytes 1572868
  5.7 8.0 %copy-start.9 = (f32[27,512]{1,0:T(8,128)S(1)}, f32[27,512]{1,0:T(8,128)}, u32[]{:S(2)}) copy-start(f32[27,512]{1,0:T(8,128)} %k_ref.7) | copy-start | bytes 165892
  5.7 8.0 %copy-start.10 = (f32[512]{0:T(512)S(1)}, f32[512]{0:T(512)}, u32[]{:S(2)}) copy-start(f32[512]{0:T(512)} %param.12) | copy-start | bytes 6148
  9.4 14.9 %collective-permute-start = (bf16[1,32,32,512]{3,2,1,0:T(8,128)(2,1)S(1)}, bf16[1,32,32,512]{3,2,1,0:T(8,128)(2,1)S(1)}, u32[]{:S(2)}, u32[]{:S(2)}) collective-permute-start(bf16[1,32,32,512]{3,2,1,0:T(8,128)(2,1)S(1)} %get-tuple-element.20), channel_id=1, source_target_pairs={{0,1},{1,0},{2,3},{3,2},{4,5},{5,4},{6,7},{7,6},{8,9},{9,8},{10,11... | collective-permute-start | bytes 3145736 | tf_op jit(solution)/shard_map/ppermute | solution.py:559
  30.6 20.1 %copy-start.2 = (bf16[512,1024]{1,0:T(8,128)(2,1)S(1)}, bf16[512,1024]{1,0:T(8,128)(2,1)}, u32[]{:S(2)}) copy-start(bf16[512,1024]{1,0:T(8,128)(2,1)} %widening_ref.1) | copy-start | bytes 3145732
  30.6 20.1 %copy-start.3 = (bf16[1024,512]{1,0:T(8,128)(2,1)S(1)}, bf16[1024,512]{1,0:T(8,128)(2,1)}, u32[]{:S(2)}) copy-start(bf16[1024,512]{1,0:T(8,128)(2,1)} %narrowing_ref.1) | copy-start | bytes 3145732
  30.6 20.1 %copy-start.4 = (bf16[512,512]{1,0:T(8,128)(2,1)S(1)}, bf16[512,512]{1,0:T(8,128)(2,1)}, u32[]{:S(2)}) copy-start(bf16[512,512]{1,0:T(8,128)(2,1)} %content_ref.1) | copy-start | bytes 1572868
  30.6 20.1 %copy-start.5 = (bf16[512,512]{1,0:T(8,128)(2,1)S(1)}, bf16[512,512]{1,0:T(8,128)(2,1)}, u32[]{:S(2)}) copy-start(bf16[512,512]{1,0:T(8,128)(2,1)} %final_ref.1) | copy-start | bytes 1572868
  30.7 20.1 %copy-start.6 = (f32[512]{0:T(512)S(1)}, f32[512]{0:T(512)}, u32[]{:S(2)}) copy-start(f32[512]{0:T(512)} %param.14) | copy-start | bytes 6148
  30.7 3.7 %collective-permute-start.2 = (bf16[8,136,128]{2,1,0:T(8,128)(2,1)S(1)}, bf16[8,136,128]{2,1,0:T(8,128)(2,1)S(1)}, u32[]{:S(2)}, u32[]{:S(2)}) collective-permute-start(bf16[8,136,128]{2,1,0:T(8,128)(2,1)S(1)} %get-tuple-element.32), channel_id=1, source_target_pairs={{0,1},{1,0},{2,3},{3,2},{4,5},{5,4},{6,7},{7,6},{8,9},{9,8},{10,11... | collective-permute-start | bytes 835592 | tf_op jit(solution)/shard_map/ppermute | solution.py:570
  33.1 30.6 %copy-start.1 = (bf16[4,32,32,512]{3,2,1,0:T(8,128)(2,1)S(1)}, bf16[4,32,32,512]{3,2,1,0:T(8,128)(2,1)}, u32[]{:S(2)}) copy-start(bf16[4,32,32,512]{3,2,1,0:T(8,128)(2,1)} %x_ref.3) | copy-start | bytes 12582916
  63.8 1.5 %collective-permute-start.3 = (bf16[256,512]{1,0:T(8,128)(2,1)S(1)}, bf16[256,512]{1,0:T(8,128)(2,1)S(1)}, u32[]{:S(2)}, u32[]{:S(2)}) collective-permute-start(bf16[256,512]{1,0:T(8,128)(2,1)S(1)} %bitcast.8), channel_id=1, source_target_pairs={{0,1},{1,0},{2,3},{3,2},{4,5},{5,4},{6,7},{7,6},{8,9},{9,8},{10,11... | collective-permute-start | bytes 786440 | tf_op jit(solution)/shard_map/ppermute | solution.py:586
